TPU v7x, 32 devices: a whole 2x2x4 slice. The times are simulated.
32 devices in a mesh: users: 8 (over z, x), rb: 4 (over y, core).
Axes of the slice: x: 2, y: 2, z: 4, core: 2. Of those that a mesh axis runs over, the one named last changes fastest.
Arguments:
- channel: bfloat16 [8192, 16, 3, 128], P('users', 'rb'), may hold values from -13 to 13
- serving: int32 [8192], P('users'), may hold values from 0 to 15, as said below
- interferers: int32 [8192, 2], P('users'), may hold values from 0 to 15, as said below
- plan: int32 [16, 16, 16], P(None, 'rb'), may hold values from 0 to 8191, as said below
- regularizer: float32 [16], P('users'), may hold values from 0.3 to 1.5
- noise_floor: float32 [16], replicated, may hold values from 0.05 to 0.5
Outputs:
- precoders: bfloat16 [16, 16, 16, 128], P('users', 'rb')
- track_metric: float32 [8192, 16], P('users', 'rb')
- entry_rate: float32 [16, 16, 16], P('users', 'rb')
Inputs may be any that keep to these rules, and one draw needn't show every extreme that they name: `serving`: each aligned block of 1024 tracks holds exactly 64 tracks served by each cell. `interferers`: A track's 2 interfering cells differ from each other and from its serving cell; each aligned block of 1024 tracks holds exactly 64 tracks with a given cell in a given column. `plan`: each entry names a track served by that cell, and the 16 tracks of a cell on one resource block differ. Take a cell group g (cells g * 2 to g * 2 + 1) and an aligned block of 4 resource blocks: at most 32 of its entries name tracks of one aligned block of 1024 tracks.
All inputs are finite; a program needn't handle non-finite values.
Results may differ from a plain program's by a relative error of at most 0.0035.
Values may be sent and summed in bfloat16 or wider, within the bound.
A program may use at most 64 MiB of HBM per device.

v0:
```python
import jax
import jax.numpy as jnp
from jax import lax
from jax.sharding import PartitionSpec as P

ITERS = 12


HIGH = lax.Precision.HIGHEST


def real_form(beam_rows):
    antennas = beam_rows.shape[-1] // 2
    turned = jnp.concatenate([beam_rows[..., antennas:], -beam_rows[..., :antennas]], axis=-1)
    return jnp.concatenate([beam_rows, turned], axis=-2)


def embed_rows(channel_rows):
    antennas = channel_rows.shape[-1] // 2
    bottom_rows = jnp.concatenate(
        [-channel_rows[..., antennas:], channel_rows[..., :antennas]], axis=-1
    )
    return jnp.concatenate([channel_rows, bottom_rows], axis=-2)


def unscaled_beams(sched_rows, regularizer):
    beam_count = sched_rows.shape[-2]
    embedded = embed_rows(sched_rows)
    gram = jnp.einsum("crkd,crjd->crkj", embedded, embedded, preferred_element_type=jnp.float32)
    identity = jnp.eye(2 * beam_count, dtype=jnp.float32)
    gram = gram + regularizer[:, None, None, None] * identity
    gram_trace = jnp.trace(gram, axis1=2, axis2=3)
    start_inverse = (2.0 / gram_trace)[:, :, None, None] * identity

    def newton_step(iteration, inverse):
        product = jnp.einsum("crkj,crjl->crkl", gram, inverse, precision=HIGH)
        return 2.0 * inverse - jnp.einsum("crkj,crjl->crkl", inverse, product, precision=HIGH)

    inverse = lax.fori_loop(0, ITERS, newton_step, start_inverse)
    return jnp.einsum(
        "crkd,crkj->crjd", embedded.astype(jnp.float32), inverse[..., :beam_count], precision=HIGH
    )


def plain_regroup(channel, send_track, send_block, my_source, my_rank, groups, capacity):
    outgoing = channel[send_track, send_block, 0].reshape(groups, capacity, channel.shape[-1])
    arrived = lax.all_to_all(outgoing, "users", split_axis=0, concat_axis=0, tiled=True)
    return arrived[my_source, my_rank]


def return_denominators(denominator, send_track, send_block, my_source, my_rank, groups, capacity):
    outgoing = denominator[send_track, send_block].reshape(groups, capacity)
    arrived = lax.all_to_all(outgoing, "users", split_axis=0, concat_axis=0, tiled=True)
    return arrived[my_source, my_rank]


def track_fold(totals, grouped_rows, piece_forms, first_cell):
    piece_cells = piece_forms.shape[0]
    rows = lax.dynamic_slice_in_dim(grouped_rows, first_cell, piece_cells, axis=1)
    projected = jnp.einsum(
        "scqrd,crkd->scqrk", rows, piece_forms, preferred_element_type=jnp.float32
    )
    energy = jnp.sum(projected * projected, axis=-1)
    current = lax.dynamic_slice_in_dim(totals, first_cell, piece_cells, axis=1)
    return lax.dynamic_update_slice_in_dim(totals, current + energy, first_cell, axis=1)


def on_device(channel, serving, interferers, plan, regularizer, noise_floor):
    track_dev, rb_dev, slot_count, row_width = channel.shape
    cell_count = plan.shape[0]
    beam_count = plan.shape[2]
    cell_dev = regularizer.shape[0]
    served = track_dev // cell_count
    groups = lax.axis_size("users")
    my_group = lax.axis_index("users")
    entries = cell_dev * rb_dev * beam_count
    capacity = 2 * entries // groups
    rb_total = rb_dev * lax.axis_size("rb")
    all_entries = plan.reshape(groups, entries)
    owned_entry = all_entries // track_dev == my_group
    position = jnp.cumsum(owned_entry.astype(jnp.int32), axis=1) - 1
    position = jnp.where(owned_entry, position, capacity)
    entry_order = lax.broadcasted_iota(jnp.int32, (groups, entries), 1)
    local_track = all_entries - my_group * track_dev
    entry_block = entry_order // beam_count % rb_dev
    slot_iota = jnp.arange(capacity, dtype=jnp.int32)
    slot_match = (position[:, None, :] == slot_iota[None, :, None]).astype(jnp.int32)
    send_track = jnp.sum(slot_match * local_track[:, None, :], axis=2).reshape(-1)
    send_block = jnp.sum(slot_match * entry_block[:, None, :], axis=2).reshape(-1)
    my_entries = lax.dynamic_slice_in_dim(all_entries, my_group, 1, axis=0)[0]
    my_source = my_entries // track_dev
    source_match = (my_source[:, None] == jnp.arange(groups, dtype=jnp.int32)[None, :]).astype(
        jnp.int32
    )
    my_rank = jnp.sum((jnp.cumsum(source_match, axis=0) - 1) * source_match, axis=1)
    sched_rows = plain_regroup(
        channel, send_track, send_block, my_source, my_rank, groups, capacity
    )
    sched_rows = sched_rows.reshape(cell_dev, rb_dev, beam_count, row_width)
    vectors = unscaled_beams(sched_rows, regularizer)
    cell_power = lax.psum(jnp.sum(vectors * vectors, axis=(1, 2, 3)), "rb")
    precoders = (vectors * lax.rsqrt(cell_power / rb_total + 1e-06)[:, None, None, None]).astype(
        jnp.bfloat16
    )
    own_forms = real_form(precoders)
    heard_cells = jnp.concatenate([serving[:, None], interferers], axis=1)
    track_iota = jnp.arange(track_dev, dtype=jnp.int32)
    slot_cells = heard_cells.T
    orders = jnp.argsort(slot_cells * track_dev + track_iota[None, :], axis=1)
    ranks = jnp.argsort(orders, axis=1)
    grouped = jnp.stack(
        [channel[orders[slot_number], :, slot_number] for slot_number in range(slot_count)]
    )
    grouped_rows = grouped.reshape(slot_count, cell_count, served, rb_dev, row_width)
    zero_powers = jnp.zeros((slot_count, cell_count, served, rb_dev), jnp.float32)
    grouped_power = track_fold(
        zero_powers,
        grouped_rows,
        real_form(lax.all_gather(precoders, "users", axis=0, tiled=True)),
        jnp.int32(0),
    )
    grouped_power = grouped_power.reshape(slot_count, track_dev, rb_dev)
    track_power = jnp.stack(
        [grouped_power[slot_number][ranks[slot_number]] for slot_number in range(slot_count)],
        axis=2,
    )
    interference = track_power[:, :, 1]
    slot_number = 2
    interference = interference + track_power[:, :, slot_number]
    floor_match = (serving[:, None] == jnp.arange(cell_count, dtype=jnp.int32)[None, :]).astype(
        jnp.float32
    )
    track_floor = jnp.sum(floor_match * noise_floor[None, :], axis=1)
    denominator = interference + track_floor[:, None]
    track_metric = jnp.log2(1.0 + track_power[:, :, 0] / denominator)
    entry_denominator = return_denominators(
        denominator, send_track, send_block, my_source, my_rank, groups, capacity
    )
    crossed = jnp.einsum(
        "crkd,crjd->crkj", sched_rows, own_forms, preferred_element_type=jnp.float32
    )
    magnitude = (
        crossed[..., :beam_count] * crossed[..., :beam_count]
        + crossed[..., beam_count:] * crossed[..., beam_count:]
    )
    identity = jnp.eye(beam_count, dtype=jnp.float32)
    signal = jnp.sum(magnitude * identity, axis=-1)
    leakage = jnp.sum(magnitude * (1.0 - identity), axis=-1)
    entry_rate = jnp.log2(
        1.0 + signal / (leakage + entry_denominator.reshape(cell_dev, rb_dev, beam_count))
    )
    return (precoders, track_metric, entry_rate)


def solution(mesh):
    return jax.shard_map(
        on_device,
        mesh=mesh,
        in_specs=(
            P("users", "rb", None, None),
            P("users"),
            P("users", None),
            P(None, "rb", None),
            P("users"),
            P(),
        ),
        out_specs=(P("users", "rb", None, None), P("users", "rb"), P("users", "rb", None)),
        check_vma=False,
    )
```

profile of v0, /device:TPU:0, one launch (start us, length us, event | category | flops | bytes accessed | tf_op | source)
XLA Modules:
  0.0 165.9 jit_solution(6319643244378103691)
XLA Ops:
  7.2 1.0 reshape.512
  9.1 2.5 %gather_fusion = bf16[256,128]{1,0:T(8,128)(2,1)} fusion(bf16[1024,4,3,128]{3,1,2,0:T(4,128)(2,1)S(1)} %copy-done, s32[256]{0:T(256)S(1)} %bitcast.88), kind=kCustom, calls=%fused_computation | custom fusion | bytes 134144 | tf_op jit(solution)/shard_map/gather | solution.py:46
  11.6 7.3 %all-to-all-start = ((bf16[8,32,128]{2,1,0:T(8,128)(2,1)}), bf16[8,32,128]{2,1,0:T(8,128)(2,1)S(1)}, u32[]{:S(2)}, u32[]{:S(2)}) async-start(bf16[8,32,128]{2,1,0:T(8,128)(2,1)} %bitcast.2), calls=%async_computation | async-start | bytes 131072 | tf_op jit(solution)/shard_map/all_to_all | solution.py:47
  18.9 1.3 fusion.24
  21.5 0.8 select_reduce_fusion.3
  22.2 0.7 broadcast_multiply_fusion.1
  23.1 5.6 %sort.34.cloned.1.call-done = (s32[3,1024]{1,0:T(4,128)}, s32[3,1024]{1,0:T(4,128)}) async-done(((s32[3,1024]{1,0:T(4,128)}, s32[3,1024]{1,0:T(4,128)}), (s32[3,1024]{1,0:T(4,128)}, s32[3,1024]{1,0:T(4,128)})) %sort.34.cloned.1.call-update) | async-done | bytes 24592 | tf_op jit(solution)/shard_map/jit(argsort)/sort | solution.py:109
  29.3 0.9 fusion.31
  30.1 8.9 %gather_fusion.4 = bf16[1024,4,128]{2,1,0:T(4,128)(2,1)} fusion(bf16[1024,4,3,128]{3,1,2,0:T(4,128)(2,1)S(1)} %copy-done, s32[1024]{0:T(1024)S(1)} %bitcast.86), kind=kCustom, calls=%fused_computation.4 | custom fusion | bytes 2105344 | tf_op jit(solution)/shard_map/gather | solution.py:112
  39.0 2.5 %copy.52 = bf16[1,16,64,4,128]{4,2,0,3,1:T(8,128)(2,1)} copy(bf16[1,16,64,4,128]{4,3,2,1,0:T(4,128)(2,1)} %bitcast.93) | data formatting | bytes 2097152 | tf_op jit(solution)/shard_map/stack | solution.py:111
  41.5 8.9 %gather_fusion.3 = bf16[1024,4,128]{2,1,0:T(4,128)(2,1)} fusion(bf16[1024,4,3,128]{3,1,2,0:T(4,128)(2,1)S(1)} %copy-done, s32[1024]{0:T(1024)S(1)} %bitcast.85), kind=kCustom, calls=%fused_computation.3 | custom fusion | bytes 2105344 | tf_op jit(solution)/shard_map/gather | solution.py:112
  50.4 2.5 %copy.51 = bf16[1,16,64,4,128]{4,2,0,3,1:T(8,128)(2,1)} copy(bf16[1,16,64,4,128]{4,3,2,1,0:T(4,128)(2,1)} %bitcast.94) | data formatting | bytes 2097152 | tf_op jit(solution)/shard_map/stack | solution.py:111
  52.9 8.9 %gather_fusion.2 = bf16[1024,4,128]{2,1,0:T(4,128)(2,1)} fusion(bf16[1024,4,3,128]{3,1,2,0:T(4,128)(2,1)S(1)} %copy-done, s32[1024]{0:T(1024)S(1)} %bitcast.84), kind=kCustom, calls=%fused_computation.2 | custom fusion | bytes 2105344 | tf_op jit(solution)/shard_map/gather | solution.py:112
  61.8 2.5 %copy.50 = bf16[1,16,64,4,128]{4,2,0,3,1:T(8,128)(2,1)} copy(bf16[1,16,64,4,128]{4,3,2,1,0:T(4,128)(2,1)} %bitcast.95) | data formatting | bytes 2097152 | tf_op jit(solution)/shard_map/stack | solution.py:111
  64.3 0.8 compare_select_fusion
  66.3 1.1 gather_fusion.1
  68.0 7.6 %while.10 = (s32[]{:T(128)}, f32[2,4,32,32]{2,3,1,0:T(8,128)S(1)}, f32[2,4,32,32]{3,2,1,0:T(8,128)S(1)}, s32[]{:T(128)}) while((s32[]{:T(128)}, f32[2,4,32,32]{2,3,1,0:T(8,128)S(1)}, f32[2,4,32,32]{3,2,1,0:T(8,128)S(1)}, s32[]{:T(128)}) %tuple.44), condition=%wide.region_7.8_spmd, body=%wide.region_6.7_spmd.sunk | while | flops 6307842 | bytes 262197 | solution.py:39
  75.9 6.3 %psum.7 = f32[2]{0:T(128)S(1)} all-reduce(f32[2]{0:T(128)S(1)} %get-tuple-element.71), channel_id=1, replica_groups=mesh['users'=8,'rb'=4] {'rb'}, use_global_device_ids=true, to_apply=%region_9.10 | all-reduce | flops 2 | bytes 16 | tf_op jit(solution)/shard_map/psum | solution.py:101
  82.3 31.1 %all_gather.3 = bf16[16,4,16,128]{3,2,1,0:T(8,128)(2,1)S(1)} all-gather(bf16[2,4,16,128]{3,2,1,0:T(8,128)(2,1)S(1)} %multiply_convert_fusion), channel_id=1, replica_groups=mesh['users'=8,'rb'=4] {'users'}, dimensions={0}, use_global_device_ids=true | all-gather | bytes 294912 | tf_op jit(solution)/shard_map/all_gather | solution.py:119
  113.6 4.5 %multiply_reduce_fusion = f32[16,4,3,64]{3,2,1,0:T(4,128)S(1)} fusion(bf16[1,16,64,4,128]{4,2,0,3,1:T(8,128)(2,1)} %copy.52, bf16[1,16,64,4,128]{4,2,0,3,1:T(8,128)(2,1)} %copy.51, bf16[1,16,64,4,128]{4,2,0,3,1:T(8,128)(2,1)} %copy.50, bf16[16,4,16,64]{3,2,1,0:T(8,128)(2,1)S(1)} %get-tuple-element.55, bf16[16,4,16,64]{3,2,1,0:T(8,128)(2,1)S(1)} %get-tuple-element.54, ...), kind=kOutput, calls=%fused_computation.18 | convolution fusion | flops 112447488 | bytes 3719168 | tf_op jit(solution)/shard_map/scqrd,crkd->scqrk/dot_general | solution.py:60
  118.2 1.1 copy.53
  119.2 1.1 copy.54
  120.3 1.1 copy.55
  121.4 5.0 %gather_fusion.5 = f32[1024,4]{1,0:T(8,128)} fusion(f32[1024,4]{1,0:T(8,128)} %bitcast.92, s32[1024]{0:T(1024)S(1)} %copy-done.3), kind=kCustom, calls=%fused_computation.5 | custom fusion | bytes 36864 | tf_op jit(solution)/shard_map/gather | solution.py:124
  126.4 5.1 %gather_fusion.6 = f32[1024,4]{1,0:T(8,128)} fusion(f32[1024,4]{1,0:T(8,128)} %bitcast.90, s32[1024]{0:T(1024)S(1)} %broadcast_clamp_fusion.1), kind=kCustom, calls=%fused_computation.6 | custom fusion | bytes 36864 | tf_op jit(solution)/shard_map/gather | solution.py:124
  131.5 5.0 %gather_fusion.7 = f32[1024,4]{1,0:T(8,128)} fusion(f32[1024,4]{1,0:T(8,128)} %bitcast.91, s32[1024]{0:T(1024)S(1)} %copy-done.2), kind=kCustom, calls=%fused_computation.7 | custom fusion | bytes 36864 | tf_op jit(solution)/shard_map/gather | solution.py:124
  136.5 2.5 %log_multiply_fusion = (f32[1024,4]{1,0:T(8,128)}, f32[1024,4]{1,0:T(8,128)}) fusion(f32[1024,4]{1,0:T(8,128)} %gather_fusion.5, f32[1024]{0:T(1024)S(1)} %select_reduce_fusion.3, f32[1024,4]{1,0:T(8,128)} %gather_fusion.6, f32[1024,4]{1,0:T(8,128)} %gather_fusion.7), kind=kLoop, calls=%fused_computation.25 | loop fusion | flops 20480 | bytes 86016 | tf_op jit(solution)/shard_map/log2 | solution.py:135
  139.0 6.5 %gather_fusion.8 = f32[256]{0:T(256)S(1)} fusion(f32[1024,4]{1,0:T(8,128)} %get-tuple-element.51, s32[256]{0:T(256)S(1)} %bitcast.89), kind=kCustom, calls=%fused_computation.8 | custom fusion | bytes 4096 | tf_op jit(solution)/shard_map/gather | solution.py:52
  146.2 4.7 %all-to-all-start.1 = ((f32[8,1,32]{2,1,0:T(1,128)}), f32[8,1,32]{2,1,0:T(1,128)S(1)}, u32[]{:S(2)}, u32[]{:S(2)}) async-start(f32[8,1,32]{2,1,0:T(1,128)} %all_to_all.12), calls=%async_computation.1 | async-start | bytes 8192 | tf_op jit(solution)/shard_map/all_to_all | solution.py:53
  151.4 1.8 %copy.56 = f32[1024,4]{0,1:T(4,128)} copy(f32[1024,4]{1,0:T(8,128)} %get-tuple-element.50) | data formatting | bytes 32768
  153.2 4.1 %all-to-all-done.1 = f32[8,1,32]{2,1,0:T(1,128)S(1)} async-done(((f32[8,1,32]{2,1,0:T(1,128)}), f32[8,1,32]{2,1,0:T(1,128)S(1)}, u32[]{:S(2)}, u32[]{:S(2)}) %all-to-all-start.1) | async-done | bytes 1056 | tf_op jit(solution)/shard_map/all_to_all | solution.py:53
  157.4 1.0 gather_fusion.9
  (90 shorter events, 14.2 us)
Async XLA Ops:
  7.2 1.9 %copy-start = (bf16[1024,4,3,128]{3,1,2,0:T(4,128)(2,1)S(1)}, bf16[1024,4,3,128]{3,1,2,0:T(4,128)(2,1)}, u32[]{:S(2)}) copy-start(bf16[1024,4,3,128]{3,1,2,0:T(4,128)(2,1)} %param.8) | copy-start | bytes 9437188
  11.6 54.7 %all-to-all-start = ((bf16[8,32,128]{2,1,0:T(8,128)(2,1)}), bf16[8,32,128]{2,1,0:T(8,128)(2,1)S(1)}, u32[]{:S(2)}, u32[]{:S(2)}) async-start(bf16[8,32,128]{2,1,0:T(8,128)(2,1)} %bitcast.2), calls=%async_computation | async-start | bytes 131072 | tf_op jit(solution)/shard_map/all_to_all | solution.py:47
  18.9 9.7 %sort.34.cloned.1.call-start = ((), (), s32[]{:S(2)}) async-start(), calls=%async_computation.2 | async-start | bytes 98336 | tf_op jit(solution)/shard_map/jit(argsort)/sort | solution.py:109
  20.9 43.4 %sort.36.cloned.1.call-start = ((), (), s32[]{:S(2)}) async-start(), calls=%async_computation.3 | async-start | bytes 98336 | tf_op jit(solution)/shard_map/jit(argsort)/sort | solution.py:110
  82.3 68.7 %copy-start.1 = (bf16[2,4,16,128]{3,2,1,0:T(8,128)(2,1)}, bf16[2,4,16,128]{3,2,1,0:T(8,128)(2,1)S(1)}, u32[]{:S(2)}) copy-start(bf16[2,4,16,128]{3,2,1,0:T(8,128)(2,1)S(1)} %multiply_convert_fusion) | copy-start | bytes 98308
  113.6 7.8 %copy-start.3 = (s32[1024]{0:T(1024)S(1)}, s32[1024]{0:T(1024)}, u32[]{:S(2)}) copy-start(s32[1024]{0:T(1024)} %broadcast_clamp_fusion.2) | copy-start | bytes 12292
  126.4 5.1 %copy-start.2 = (s32[1024]{0:T(1024)S(1)}, s32[1024]{0:T(1024)}, u32[]{:S(2)}) copy-start(s32[1024]{0:T(1024)} %broadcast_clamp_fusion) | copy-start | bytes 12292
  146.2 11.1 %all-to-all-start.1 = ((f32[8,1,32]{2,1,0:T(1,128)}), f32[8,1,32]{2,1,0:T(1,128)S(1)}, u32[]{:S(2)}, u32[]{:S(2)}) async-start(f32[8,1,32]{2,1,0:T(1,128)} %all_to_all.12), calls=%async_computation.1 | async-start | bytes 8192 | tf_op jit(solution)/shard_map/all_to_all | solution.py:53
Sparse Core Ops, SparseCore 0:
  22.8 5.5 sort.38.cloned.1.call-done
  31.7 4.3 sort.40.cloned.1.call-done
  (2 shorter events, 0.0 us)
where the time goes:
time: 168 us; the launch traced here: 166 us
  local copies, waits for them, and re-layouts  74.6 us (44%)
  blocking collectives  37.4 us (22%)
  between operations  14.2 us (8%)
  matrix products  12.4 us (7%)
  starting transfers between devices  12 us (7%)
  other arithmetic  10.8 us (6%)
  waiting for transfers between devices  4.12 us (2%)
    all_gather x1, blocking collectives, on_device(): lax.all_gather(precoders, 'users', axis=0, tiled=True)  31.1 us
    gather x3, local copies, waits for them, and re-layouts, on_device(): channel[orders[slot_number], :, slot_number]  26.6 us
    gather x3, local copies, waits for them, and re-layouts, on_device(): grouped_power[slot_number][ranks[slot_number]]  15.1 us
    another operation x3, local copies, waits for them, and re-layouts, on_device(): jnp.stack([channel[orders[slot_number], :, slot_number] for slot_number i...  7.53 us
    all_to_all x1, starting transfers between devices, plain_regroup(): lax.all_to_all(outgoing, 'users', split_axis=0, concat_axis=0, tiled=True)  7.25 us
    gather x1, local copies, waits for them, and re-layouts, return_denominators(): outgoing = denominator[send_track, send_block].reshape(groups, capacity)  6.5 us
    psum x1, blocking collectives, on_device(): cell_power = lax.psum(jnp.sum(vectors * vectors, axis=(1, 2, 3)), 'rb')  6.3 us
    sort x2, local copies, waits for them, and re-layouts, on_device(): orders = jnp.argsort(slot_cells * track_dev + track_iota[None, :], axis=1)  5.59 us
  transfers between devices with their start and end apart: 2, of which 1 were waited for; matrix products, arithmetic and copies ran while one was open for 26% of the time, Pallas kernels for 0%

commit v1 on v0

v1 whole, which is shorter than its diff:
```python
import functools

import jax
import jax.numpy as jnp
from jax import lax
from jax.experimental import pallas as pl
from jax.experimental.pallas import tpu as pltpu
from jax.sharding import PartitionSpec as P

ITERS = 12
F32 = jnp.float32
BF16 = jnp.bfloat16
HIGH = lax.Precision.HIGHEST


def iota(shape, dim):
    return lax.broadcasted_iota(jnp.int32, shape, dim)


def log2_of(n):
    assert n & (n - 1) == 0
    return n.bit_length() - 1


def turn(rows):
    half = rows.shape[-1] // 2
    sign = jnp.where(iota(rows.shape, 1) < half, 1.0, -1.0)
    return pltpu.roll(rows, half, 1) * sign


def dot_nt(a, b):
    return lax.dot_general(a, b, (((1,), (1,)), ((), ())), preferred_element_type=F32)


def dot_nn(a, b):
    return jnp.dot(a, b, preferred_element_type=F32)


def split3(x):
    high = x.astype(BF16)
    rest = x - high.astype(F32)
    middle = rest.astype(BF16)
    return high, middle, (rest - middle.astype(F32)).astype(BF16)


def dot_split(x, b):
    high, middle, low = split3(x)
    return dot_nn(low, b) + dot_nn(middle, b) + dot_nn(high, b)


def spread(a, beams):
    lane = iota(a.shape, 1)
    base = lane - (lane & (beams - 1))
    return lambda m: jnp.take_along_axis(a, base + m, axis=1, mode="promise_in_bounds")


def complex_product(left_r, left_i, right_r, right_i, beams):
    out_r = out_i = None
    for m in range(beams):
        lr, li = left_r(m), left_i(m)
        rr, ri = right_r[m : m + 1, :], right_i[m : m + 1, :]
        term_r = lr * rr - li * ri
        term_i = lr * ri + li * rr
        out_r = term_r if out_r is None else out_r + term_r
        out_i = term_i if out_i is None else out_i + term_i
    return out_r, out_i


def newton_inverse(gram_r, gram_i, reg_lanes, beams):
    shape = gram_r.shape
    lanes = shape[1]
    shift = log2_of(beams)
    diagonal = (iota(shape, 1) & (beams - 1)) == iota(shape, 0)
    gram_r = gram_r + jnp.where(diagonal, reg_lanes, 0.0)
    diag_row = jnp.sum(jnp.where(diagonal, gram_r, 0.0), axis=0, keepdims=True)
    same = (iota((lanes, lanes), 0) >> shift) == (iota((lanes, lanes), 1) >> shift)
    trace = jnp.dot(
        jnp.broadcast_to(diag_row, (8, lanes)),
        jnp.where(same, 1.0, 0.0),
        precision=HIGH,
        preferred_element_type=F32,
    )[0:1, :]
    start_r = jnp.where(diagonal, 1.0 / trace, 0.0)
    start_i = jnp.zeros(shape, F32)
    gather_r, gather_i = spread(gram_r, beams), spread(gram_i, beams)
    held_r = [gather_r(m) for m in range(beams)]
    held_i = [gather_i(m) for m in range(beams)]

    def step(_, carry):
        xr, xi = carry
        yr, yi = complex_product(lambda m: held_r[m], lambda m: held_i[m], xr, xi, beams)
        zr, zi = complex_product(spread(xr, beams), spread(xi, beams), yr, yi, beams)
        return 2.0 * xr - zr, 2.0 * xi - zi

    return lax.fori_loop(0, ITERS, step, (start_r, start_i))


def kernel(
    dims,
    ch_ref,
    ent_ref,
    cells_ref,
    reg_ref,
    noise_ref,
    prec_ref,
    metric_ref,
    rate_ref,
    wide,
    planes,
    out_rows,
    in_rows,
    own_w,
    all_w,
    forms,
    received,
    pw_own,
    pw_in,
    dn_own,
    dn_in,
    row_send,
    row_recv,
    w_send,
    w_recv,
    pw_send,
    pw_recv,
    dn_send,
    dn_recv,
):
    groups, rb_groups, tracks, blocks, slots, cells, beams, cell_dev, capacity = dims
    entries = cell_dev * blocks * beams
    width = ch_ref.shape[1]
    track_shift = log2_of(tracks)
    beam_shift = log2_of(beams)
    me = lax.axis_index("users")
    my_rb = lax.axis_index("rb")

    barrier = pltpu.get_barrier_semaphore()
    for offset in range(1, groups):
        pl.semaphore_signal(
            barrier, inc=1, device_id={"users": lax.rem(me + offset, groups)},
            device_id_type=pl.DeviceIdType.MESH,
        )
    for offset in range(1, rb_groups):
        pl.semaphore_signal(
            barrier, inc=1, device_id={"rb": lax.rem(my_rb + offset, rb_groups)},
            device_id_type=pl.DeviceIdType.MESH,
        )

    def user_copy(src, dst, send, recv, offset):
        return pltpu.make_async_remote_copy(
            src_ref=src,
            dst_ref=dst,
            send_sem=send.at[offset],
            recv_sem=recv.at[offset],
            device_id={"users": lax.rem(me + offset, groups)},
            device_id_type=pl.DeviceIdType.MESH,
        )

    stride = slots * blocks
    rows = ch_ref.shape[0]
    chunk = rows // 8

    def widen(i, carry):
        part = pl.ds(pl.multiple_of(i * chunk, chunk), chunk)
        wide[part, :] = ch_ref[part, :].astype(F32)
        return carry

    lax.fori_loop(0, 8, widen, 0)

    def extract(slot):
        for block in range(blocks):
            number = slot * blocks + block
            planes[number] = wide[pl.ds(number, tracks, stride=stride), :].astype(BF16)

    extract(0)

    ent = ent_ref[...]
    owner = ent >> track_shift
    lane_e = iota((1, entries), 1)
    block_e = (lane_e >> beam_shift) & (blocks - 1)
    code = ((ent & (tracks - 1)) + block_e * tracks + 1).astype(F32)
    before = jnp.where(iota((entries, entries), 0) < iota((entries, entries), 1), 1.0, 0.0).astype(BF16)
    mine = jnp.where(owner == me, 1.0, 0.0)
    rank = dot_nn(mine.astype(BF16), before)
    slot_number = iota((capacity, entries), 0).astype(F32)

    def hits_of(flags, ranks, group):
        keep = flags[group : group + 1, :]
        return jnp.where(ranks[group : group + 1, :] == slot_number, keep, 0.0)

    sends = [hits_of(mine, rank, group) for group in range(groups)]
    picks = jnp.concatenate(
        [
            jnp.sum(sends[group] * code[group : group + 1, :], axis=1, keepdims=True)
            for group in range(groups)
        ],
        axis=0,
    ).astype(jnp.int32) - 1
    track_lane = iota((groups * capacity, tracks), 1)
    gathered = None
    for block in range(blocks):
        one_hot = jnp.where(picks - block * tracks == track_lane, 1.0, 0.0).astype(BF16)
        part = dot_nn(one_hot, planes[block])
        gathered = part if gathered is None else gathered + part
    for group in range(groups):
        out_rows[group] = gathered[group * capacity : (group + 1) * capacity].astype(BF16)

    pl.semaphore_wait(barrier, groups - 1 + rb_groups - 1)

    row_copies = []
    for offset in range(1, groups):
        dst = lax.rem(me + offset, groups)
        copy = user_copy(out_rows.at[dst], in_rows.at[me], row_send, row_recv, offset)
        copy.start()
        row_copies.append(copy)
    in_rows[pl.ds(me, 1)] = out_rows[pl.ds(me, 1)]

    for slot in range(1, slots):
        extract(slot)

    is_me = iota(ent.shape, 0) == me
    my_owner = jnp.sum(jnp.where(is_me, owner.astype(F32), 0.0), axis=0, keepdims=True)
    from_src = jnp.where(my_owner == iota(ent.shape, 0).astype(F32), 1.0, 0.0)
    src_rank = dot_nn(from_src.astype(BF16), before)
    arrivals = jnp.concatenate(
        [hits_of(from_src, src_rank, group) for group in range(groups)], axis=0
    )
    place = jnp.transpose(arrivals).astype(BF16)

    for copy in row_copies:
        copy.wait_recv()
    came = jnp.concatenate([in_rows[group].astype(F32) for group in range(groups)], axis=0)
    sched = dot_nn(place, came.astype(BF16))
    sched_b = sched.astype(BF16)
    turned_b = turn(sched).astype(BF16)

    full_r = dot_nt(sched_b, sched_b)
    full_i = dot_nt(sched_b, turned_b)
    shape = (beams, entries)
    lane_problem = iota(shape, 1) >> beam_shift
    gram_r = gram_i = jnp.zeros(shape, F32)
    for problem in range(cell_dev * blocks):
        part = slice(problem * beams, (problem + 1) * beams)
        here = lane_problem == problem
        gram_r = gram_r + jnp.where(here, full_r[part, :], 0.0)
        gram_i = gram_i + jnp.where(here, full_i[part, :], 0.0)
    reg_lanes = jnp.zeros((1, entries), F32)
    cell_lanes = blocks * beams
    for cell in range(cell_dev):
        reg_lanes = jnp.where(lane_e >= cell * cell_lanes, reg_ref[cell], reg_lanes)
    inv_r, inv_i = newton_inverse(gram_r, gram_i, reg_lanes, beams)

    problems = cell_dev * blocks
    square = (entries, entries)
    same = (iota(square, 0) >> beam_shift) == (iota(square, 1) >> beam_shift)
    wide_r = jnp.where(same, jnp.concatenate([inv_r] * problems, axis=0), 0.0)
    wide_i = jnp.where(same, jnp.concatenate([inv_i] * problems, axis=0), 0.0)
    vectors = dot_split(wide_r, sched_b) + dot_split(wide_i, turned_b)

    squares = vectors * vectors
    sums = [
        jnp.sum(squares[cell * cell_lanes : (cell + 1) * cell_lanes], axis=0, keepdims=True)
        for cell in range(cell_dev)
    ]
    pw_own[...] = jnp.concatenate(sums + [jnp.zeros((8 - cell_dev, width), F32)], axis=0)
    pw_copies = []
    for offset in range(1, rb_groups):
        copy = pltpu.make_async_remote_copy(
            src_ref=pw_own,
            dst_ref=pw_in.at[my_rb],
            send_sem=pw_send.at[offset],
            recv_sem=pw_recv.at[offset],
            device_id={"rb": lax.rem(my_rb + offset, rb_groups)},
            device_id_type=pl.DeviceIdType.MESH,
        )
        copy.start()
        pw_copies.append(copy)
    pw_in[pl.ds(my_rb, 1)] = pw_own[...][None]
    for copy in pw_copies:
        copy.wait_recv()
    total = jnp.sum(jnp.sum(pw_in[...], axis=0), axis=1, keepdims=True)
    scale = lax.rsqrt(total / (blocks * rb_groups) + 1e-06)
    scaled = jnp.concatenate(
        [
            vectors[cell * cell_lanes : (cell + 1) * cell_lanes] * scale[cell : cell + 1, :]
            for cell in range(cell_dev)
        ],
        axis=0,
    )
    prec = scaled.astype(BF16)
    own_w[...] = prec
    w_copies = []
    for offset in range(1, groups):
        copy = user_copy(own_w, all_w.at[me], w_send, w_recv, offset)
        copy.start()
        w_copies.append(copy)
    all_w[pl.ds(me, 1)] = prec[None]
    prec_ref[...] = prec

    prec_turned = turn(prec.astype(F32)).astype(BF16)
    z_r = dot_nt(prec, sched_b)
    z_i = dot_nt(prec_turned, sched_b)
    magnitude = jnp.where(same, z_r * z_r + z_i * z_i, 0.0)
    on_diagonal = iota(square, 0) == iota(square, 1)
    signal = jnp.sum(jnp.where(on_diagonal, magnitude, 0.0), axis=0, keepdims=True)
    leakage = jnp.sum(jnp.where(on_diagonal, 0.0, magnitude), axis=0, keepdims=True)

    for copy in w_copies:
        copy.wait_recv()

    count = cells * beams
    cell_shift = log2_of(cells)
    new_row = iota((count, count), 0)
    old_row = ((new_row & (cells - 1)) << beam_shift) + (new_row >> cell_shift)
    order = jnp.where(old_row == iota((count, count), 1), 1.0, 0.0).astype(BF16)
    for block in range(blocks):
        stacked = jnp.concatenate(
            [
                all_w[
                    group,
                    cell * cell_lanes + block * beams : cell * cell_lanes + (block + 1) * beams,
                    :,
                ]
                for group in range(groups)
                for cell in range(cell_dev)
            ],
            axis=0,
        )
        ordered = dot_nn(order, stacked)
        forms[block, 0:count, :] = ordered.astype(BF16)
        forms[block, count : 2 * count, :] = turn(ordered).astype(BF16)

    cell_row = iota((cells, tracks), 0)

    def track_powers(number, carry):
        slot, block = number // blocks, number % blocks
        projected = dot_nt(forms[block], planes[number])
        energy = jnp.sum((projected * projected).reshape(2 * beams, cells, tracks), axis=0)
        heard = cells_ref[slot]
        received[number] = jnp.sum(
            jnp.where(cell_row == heard, energy, 0.0), axis=0, keepdims=True
        )
        return carry

    lax.fori_loop(0, slots * blocks, track_powers, 0)

    floor = jnp.zeros((1, tracks), F32)
    serving = cells_ref[0]
    for cell in range(cells):
        floor = jnp.where(serving == cell, noise_ref[cell], floor)
    denominators = []
    for block in range(blocks):
        interference = received[blocks + block]
        for slot in range(2, slots):
            interference = interference + received[slot * blocks + block]
        denominators.append(interference + floor)
    power = jnp.concatenate([received[block] for block in range(blocks)], axis=0)
    all_denominators = jnp.concatenate(denominators, axis=0)

    found = jnp.zeros((groups * capacity, tracks), F32)
    for block in range(blocks):
        found = jnp.where(picks - block * tracks == track_lane, denominators[block], found)
    column = jnp.sum(found, axis=1, keepdims=True)
    dn_own[...] = jnp.concatenate(
        [
            jnp.sum(
                sends[group] * column[group * capacity : (group + 1) * capacity],
                axis=0,
                keepdims=True,
            )
            for group in range(groups)
        ],
        axis=0,
    )
    dn_copies = []
    for offset in range(1, groups):
        copy = user_copy(dn_own, dn_in.at[me], dn_send, dn_recv, offset)
        copy.start()
        dn_copies.append(copy)
    dn_in[pl.ds(me, 1)] = dn_own[...][None]

    metric_ref[...] = jnp.log2(1.0 + power / all_denominators)

    for copy in dn_copies:
        copy.wait_recv()
    every = jnp.sum(dn_in[...], axis=0)
    entry_denominator = jnp.sum(jnp.where(is_me, every, 0.0), axis=0, keepdims=True)
    rate_ref[...] = jnp.log2(1.0 + signal / (leakage + entry_denominator))

    for copy in row_copies + pw_copies + w_copies + dn_copies:
        copy.wait_send()


def on_device(channel, serving, interferers, plan, regularizer, noise_floor):
    tracks, blocks, slots, width = channel.shape
    cells, _, beams = plan.shape
    cell_dev = regularizer.shape[0]
    groups = lax.axis_size("users")
    rb_groups = lax.axis_size("rb")
    entries = cell_dev * blocks * beams
    capacity = 2 * entries // groups
    dims = (groups, rb_groups, tracks, blocks, slots, cells, beams, cell_dev, capacity)
    rows = channel.transpose(0, 2, 1, 3).reshape(tracks * slots * blocks, width)
    heard = jnp.concatenate([serving[None, :], interferers.T], axis=0)[:, None, :]
    vmem = pl.BlockSpec(memory_space=pltpu.VMEM)
    smem = pl.BlockSpec(memory_space=pltpu.SMEM)
    dma = pltpu.SemaphoreType.DMA
    precoders, metric, rate = pl.pallas_call(
        functools.partial(kernel, dims),
        out_shape=(
            jax.ShapeDtypeStruct((entries, width), BF16),
            jax.ShapeDtypeStruct((blocks, tracks), F32),
            jax.ShapeDtypeStruct((1, entries), F32),
        ),
        in_specs=[vmem, vmem, vmem, smem, smem],
        out_specs=(vmem, vmem, vmem),
        scratch_shapes=[
            pltpu.VMEM((tracks * slots * blocks, width), F32),
            pltpu.VMEM((slots * blocks, tracks, width), BF16),
            pltpu.VMEM((groups, capacity, width), BF16),
            pltpu.VMEM((groups, capacity, width), BF16),
            pltpu.VMEM((entries, width), BF16),
            pltpu.VMEM((groups, entries, width), BF16),
            pltpu.VMEM((blocks, 2 * cells * beams, width), BF16),
            pltpu.VMEM((slots * blocks, 1, tracks), F32),
            pltpu.VMEM((8, width), F32),
            pltpu.VMEM((rb_groups, 8, width), F32),
            pltpu.VMEM((groups, entries), F32),
            pltpu.VMEM((groups, groups, entries), F32),
            dma((groups,)),
            dma((groups,)),
            dma((groups,)),
            dma((groups,)),
            dma((rb_groups,)),
            dma((rb_groups,)),
            dma((groups,)),
            dma((groups,)),
        ],
        compiler_params=pltpu.CompilerParams(
            collective_id=0, has_side_effects=True, vmem_limit_bytes=48 << 20
        ),
    )(rows, plan.reshape(groups, entries), heard, regularizer, noise_floor)
    return (
        precoders.reshape(cell_dev, blocks, beams, width),
        metric.T,
        rate.reshape(cell_dev, blocks, beams),
    )


def solution(mesh):
    return jax.shard_map(
        on_device,
        mesh=mesh,
        in_specs=(
            P("users", "rb", None, None),
            P("users"),
            P("users", None),
            P(None, "rb", None),
            P("users"),
            P(),
        ),
        out_specs=(P("users", "rb", None, None), P("users", "rb"), P("users", "rb", None)),
        check_vma=False,
    )
```

time: 168 us -> 43.9 us (0.26); the launches traced: 166 us -> 43.6 us
  local copies, waits for them, and re-layouts: 74.6 us -> 6.47 us
  blocking collectives: 37.4 us -> 0 us
  Pallas kernels: 0 us -> 35.1 us
  between operations: 14.2 us -> 0.66 us
  matrix products: 12.4 us -> 0 us
  starting transfers between devices: 12 us -> 0 us
  other arithmetic: 10.8 us -> 1.38 us
  waiting for transfers between devices: 4.12 us -> 0 us
    gather x10 -> x0, local copies, waits for them, and re-layouts: 52.9 us -> none  [the longest x3 26.6 us: on_device(): channel[orders[slot_number], :, slot_number]]
    pallas_call x0 -> x1, Pallas kernels: none -> 35.1 us  [on_device(): pl.pallas_call(functools.partial(kernel, dims), out_shape=(jax.ShapeDtype...]
    all_gather x1 -> x0, blocking collectives: 31.1 us -> none  [on_device(): lax.all_gather(precoders, 'users', axis=0, tiled=True)]
    dot_general x28 -> x0, matrix products: 12.4 us -> none  [the longest x1 4.47 us: track_fold(): jnp.einsum('scqrd,crkd->scqrk', rows, piece_forms, preferred_element_type...]
    all_to_all x2 -> x0, starting transfers between devices: 12 us -> none  [the longest x1 7.25 us: plain_regroup(): lax.all_to_all(outgoing, 'users', split_axis=0, concat_axis=0, tiled=True)]
    another operation x3 -> x0, local copies, waits for them, and re-layouts: 7.53 us -> none  [on_device(): jnp.stack([channel[orders[slot_number], :, slot_number] for slot_number i...]
    psum x1 -> x0, blocking collectives: 6.3 us -> none  [on_device(): cell_power = lax.psum(jnp.sum(vectors * vectors, axis=(1, 2, 3)), 'rb')]
    sort x4 -> x0, local copies, waits for them, and re-layouts: 5.64 us -> none  [the longest x2 5.59 us: on_device(): orders = jnp.argsort(slot_cells * track_dev + track_iota[None, :], axis=1)]
  transfers between devices with their start and end apart: 2 -> 0, of which waited for: 1 -> 0; matrix products, arithmetic and copies ran while one was open for 26% -> 0% of each run, Pallas kernels for 0% -> 0%
where the time goes in v1:
time: 43.9 us; the launch traced here: 43.6 us
  Pallas kernels  35.1 us (80%)
  local copies, waits for them, and re-layouts  6.47 us (15%)
  other arithmetic  1.38 us (3%)
  between operations  0.66 us (2%)
    pallas_call x1, Pallas kernels, on_device(): pl.pallas_call(functools.partial(kernel, dims), out_shape=(jax.ShapeDtype...  35.1 us
    unnamed x8, local copies, waits for them, and re-layouts  4.41 us

profile of v1, /device:TPU:0, one launch (start us, length us, event | category | flops | bytes accessed | tf_op | source)
XLA Modules:
  0.0 43.6 jit_solution(4274656966635003231)
XLA Ops:
  0.6 0.8 %reshape.19.ent_ref = s32[8,128]{1,0:T(8,128)S(1)} reshape(s32[16,4,16]{2,1,0:T(4,128)} %param.9) | data formatting | bytes 8192 | tf_op jit(solution)/shard_map/reshape | solution.py:442
  1.5 0.7 %pad_add_fusion = s32[3,1024]{1,0:T(4,128)S(1)} fusion(s32[2,1024]{1,0:T(2,128)} %bitcast.10, s32[1,1024]{1,0:T(1,128)} %bitcast.11), kind=kLoop, calls=%fused_computation | loop fusion | flops 3072 | bytes 24576 | tf_op jit(solution)/shard_map/concatenate | solution.py:404
  2.2 0.0 copy-start
  2.2 1.9 %copy-done = bf16[1024,4,3,128]{3,1,2,0:T(4,128)(2,1)S(1)} copy-done((bf16[1024,4,3,128]{3,1,2,0:T(4,128)(2,1)S(1)}, bf16[1024,4,3,128]{3,1,2,0:T(4,128)(2,1)}, u32[]{:S(2)}) %copy-start) | copy-done | bytes 3145752
  4.1 0.0 copy-start.1
  4.1 0.7 %copy-done.1 = f32[2]{0:T(128)S(1)} copy-done((f32[2]{0:T(128)S(1)}, f32[2]{0:T(128)}, u32[]{:S(2)}) %copy-start.1) | copy-done | bytes 32
  4.8 0.0 copy-start.2
  4.8 0.7 %copy-done.2 = f32[16]{0:T(128)S(1)} copy-done((f32[16]{0:T(128)S(1)}, f32[16]{0:T(128)}, u32[]{:S(2)}) %copy-start.2) | copy-done | bytes 88
  5.4 35.1 %shard_map.85 = (bf16[128,128]{1,0:T(8,128)(2,1)S(1)}, f32[4,1024]{1,0:T(4,128)S(1)}, f32[1,128]{1,0:T(1,128)S(1)}) custom-call(bf16[12288,128]{1,0:T(8,128)(2,1)S(1)} %bitcast.7, s32[8,128]{1,0:T(8,128)S(1)} %reshape.19.ent_ref, s32[3,1,1024]{2,1,0:T(1,128)S(1)} %broadcast_in_dim.7.cells_ref, f32[2]{0:T(128)S(1)} %copy-done.1, f32[16]{0:T(128)S(1)} %copy-done.2), custom_call_target="tpu_custom_call" | custom-call | tf_op jit(solution)/shard_map/pallas_call | solution.py:408
  40.5 0.5 %broadcast.3 = f32[]{:T(128)} broadcast(f32[]{:T(128)} %constant.6), dimensions={} | broadcast | bytes 8 | tf_op jit(solution)/shard_map/pallas_call | solution.py:408
  41.0 0.7 %reduce.3 = f32[128]{0:T(128)S(1)} reduce(f32[1,128]{1,0:T(1,128)S(1)} %get-tuple-element.8, f32[]{:T(128)} %broadcast.3), dimensions={0}, to_apply=%get-tuple-element.8.reduce_sub_computation.3 | reduce | bytes 1028 | tf_op jit(solution)/shard_map/pallas_call | solution.py:408
  41.7 0.7 %reshape.21 = f32[2,4,16]{2,1,0:T(4,128)} reshape(f32[128]{0:T(128)S(1)} %reduce.3) | data formatting | bytes 1024 | tf_op jit(solution)/shard_map/reshape | solution.py:446
  42.4 0.6 %copy.11 = bf16[2,4,16,128]{3,2,1,0:T(8,128)(2,1)} copy(bf16[2,4,16,128]{3,2,1,0:T(8,128)(2,1)S(1)} %bitcast.8) | data formatting | bytes 65536
  43.0 0.6 %copy.12 = f32[1024,4]{0,1:T(4,128)} copy(f32[1024,4]{0,1:T(4,128)S(1)} %bitcast.9) | data formatting | bytes 32768
  (1 shorter events, 0.0 us)
Async XLA Ops:
  2.2 1.9 %copy-start = (bf16[1024,4,3,128]{3,1,2,0:T(4,128)(2,1)S(1)}, bf16[1024,4,3,128]{3,1,2,0:T(4,128)(2,1)}, u32[]{:S(2)}) copy-start(bf16[1024,4,3,128]{3,1,2,0:T(4,128)(2,1)} %param.6) | copy-start | bytes 9437188
  4.1 0.7 %copy-start.1 = (f32[2]{0:T(128)S(1)}, f32[2]{0:T(128)}, u32[]{:S(2)}) copy-start(f32[2]{0:T(128)} %reg_ref.1) | copy-start | bytes 28
  4.8 0.7 %copy-start.2 = (f32[16]{0:T(128)S(1)}, f32[16]{0:T(128)}, u32[]{:S(2)}) copy-start(f32[16]{0:T(128)} %noise_ref.1) | copy-start | bytes 196

commit v2 on v1

--- a/solution.py
+++ b/solution.py
@@ -95,16 +95,36 @@
     return lax.fori_loop(0, ITERS, step, (start_r, start_i))
 
 
+def flip(index, mask, count):
+    result = 0
+    bit = 1
+    while bit < count:
+        digit = lax.rem(lax.div(index, bit), 2)
+        result = result + bit * (1 - digit if mask & bit else digit)
+        bit *= 2
+    return result
+
+
 def kernel(
     dims,
-    ch_ref,
-    ent_ref,
+    ch_hbm,
+    plan_hbm,
+    serving_hbm,
+    inter_hbm,
+    reg_hbm,
+    noise_hbm,
+    prec_out,
+    metric_out,
+    rate_out,
+    prec_ref,
+    metric_ref,
+    rate_ref,
+    raw,
+    plan_ref,
+    inter_ref,
     cells_ref,
     reg_ref,
     noise_ref,
-    prec_ref,
-    metric_ref,
-    rate_ref,
     wide,
     planes,
     out_rows,
@@ -115,34 +135,60 @@
     received,
     pw_own,
     pw_in,
+    sc_own,
+    sc_in,
     dn_own,
     dn_in,
+    load_sem,
+    small_sem,
+    store_sem,
     row_send,
     row_recv,
     w_send,
     w_recv,
     pw_send,
     pw_recv,
+    sc_send,
+    sc_recv,
     dn_send,
     dn_recv,
 ):
     groups, rb_groups, tracks, blocks, slots, cells, beams, cell_dev, capacity = dims
     entries = cell_dev * blocks * beams
-    width = ch_ref.shape[1]
+    width = raw.shape[1]
     track_shift = log2_of(tracks)
     beam_shift = log2_of(beams)
     me = lax.axis_index("users")
     my_rb = lax.axis_index("rb")
 
+    rows = raw.shape[0]
+    pieces = load_sem.shape[0]
+    chunk = rows // pieces
+    loads = []
+    small = [
+        pltpu.make_async_copy(plan_hbm, plan_ref, small_sem.at[0]),
+        pltpu.make_async_copy(serving_hbm, cells_ref.at[0], small_sem.at[1]),
+        pltpu.make_async_copy(inter_hbm, inter_ref, small_sem.at[2]),
+        pltpu.make_async_copy(reg_hbm, reg_ref, small_sem.at[3]),
+        pltpu.make_async_copy(noise_hbm, noise_ref, small_sem.at[4]),
+    ]
+    for copy in small:
+        copy.start()
+    for i in range(pieces):
+        part = pl.ds(i * chunk, chunk)
+        copy = pltpu.make_async_copy(ch_hbm.at[part], raw.at[part], load_sem.at[i])
+        copy.start()
+        loads.append(copy)
+
     barrier = pltpu.get_barrier_semaphore()
     for offset in range(1, groups):
         pl.semaphore_signal(
-            barrier, inc=1, device_id={"users": lax.rem(me + offset, groups)},
+            barrier, inc=1, device_id={"users": flip(me, offset, groups)},
             device_id_type=pl.DeviceIdType.MESH,
         )
     for offset in range(1, rb_groups):
         pl.semaphore_signal(
-            barrier, inc=1, device_id={"rb": lax.rem(my_rb + offset, rb_groups)},
+            barrier, inc=1, device_id={"rb": flip(my_rb, offset, rb_groups)},
             device_id_type=pl.DeviceIdType.MESH,
         )
 
@@ -152,34 +198,42 @@
             dst_ref=dst,
             send_sem=send.at[offset],
             recv_sem=recv.at[offset],
-            device_id={"users": lax.rem(me + offset, groups)},
+            device_id={"users": flip(me, offset, groups)},
             device_id_type=pl.DeviceIdType.MESH,
         )
 
-    stride = slots * blocks
-    rows = ch_ref.shape[0]
-    chunk = rows // 8
-
-    def widen(i, carry):
-        part = pl.ds(pl.multiple_of(i * chunk, chunk), chunk)
-        wide[part, :] = ch_ref[part, :].astype(F32)
-        return carry
-
-    lax.fori_loop(0, 8, widen, 0)
-
-    def extract(slot):
-        for block in range(blocks):
-            number = slot * blocks + block
-            planes[number] = wide[pl.ds(number, tracks, stride=stride), :].astype(BF16)
-
-    extract(0)
-
-    ent = ent_ref[...]
+    for copy in small:
+        copy.wait()
+    for slot in range(1, slots):
+        cells_ref[slot] = inter_ref[slot - 1 : slot, :]
+    cell_lanes = blocks * beams
+    spread_plan = None
+    for block in range(blocks):
+        lane = iota((beams, entries), 1) & (cell_lanes - 1)
+        put = jnp.where(lane == iota((beams, entries), 0) + block * beams, 1.0, 0.0)
+        part = jnp.dot(
+            plan_ref[:, block, :].astype(F32), put, precision=HIGH, preferred_element_type=F32
+        )
+        spread_plan = part if spread_plan is None else spread_plan + part
+    ent_f = jnp.zeros((groups, entries), F32)
+    for cell in range(cell_dev):
+        pick = jnp.where(
+            iota((groups, cells), 1) == cell_dev * iota((groups, cells), 0) + cell, 1.0, 0.0
+        )
+        lane = iota((cells, entries), 1)
+        in_cell = (lane >= cell * cell_lanes) & (lane < (cell + 1) * cell_lanes)
+        ent_f = ent_f + jnp.dot(
+            pick, jnp.where(in_cell, spread_plan, 0.0), precision=HIGH, preferred_element_type=F32
+        )
+    ent = ent_f.astype(jnp.int32)
+
     owner = ent >> track_shift
     lane_e = iota((1, entries), 1)
     block_e = (lane_e >> beam_shift) & (blocks - 1)
     code = ((ent & (tracks - 1)) + block_e * tracks + 1).astype(F32)
-    before = jnp.where(iota((entries, entries), 0) < iota((entries, entries), 1), 1.0, 0.0).astype(BF16)
+    before = jnp.where(
+        iota((entries, entries), 0) < iota((entries, entries), 1), 1.0, 0.0
+    ).astype(BF16)
     mine = jnp.where(owner == me, 1.0, 0.0)
     rank = dot_nn(mine.astype(BF16), before)
     slot_number = iota((capacity, entries), 0).astype(F32)
@@ -196,6 +250,20 @@
         ],
         axis=0,
     ).astype(jnp.int32) - 1
+
+    stride = slots * blocks
+    for i in range(pieces):
+        loads[i].wait()
+        part = slice(i * chunk, (i + 1) * chunk)
+        wide[part, :] = raw[part, :].astype(F32)
+
+    def extract(slot):
+        for block in range(blocks):
+            number = slot * blocks + block
+            planes[number] = wide[pl.ds(number, tracks, stride=stride), :].astype(BF16)
+
+    extract(0)
+
     track_lane = iota((groups * capacity, tracks), 1)
     gathered = None
     for block in range(blocks):
@@ -209,7 +277,7 @@
 
     row_copies = []
     for offset in range(1, groups):
-        dst = lax.rem(me + offset, groups)
+        dst = flip(me, offset, groups)
         copy = user_copy(out_rows.at[dst], in_rows.at[me], row_send, row_recv, offset)
         copy.start()
         row_copies.append(copy)
@@ -245,7 +313,6 @@
         gram_r = gram_r + jnp.where(here, full_r[part, :], 0.0)
         gram_i = gram_i + jnp.where(here, full_i[part, :], 0.0)
     reg_lanes = jnp.zeros((1, entries), F32)
-    cell_lanes = blocks * beams
     for cell in range(cell_dev):
         reg_lanes = jnp.where(lane_e >= cell * cell_lanes, reg_ref[cell], reg_lanes)
     inv_r, inv_i = newton_inverse(gram_r, gram_i, reg_lanes, beams)
@@ -256,6 +323,15 @@
     wide_r = jnp.where(same, jnp.concatenate([inv_r] * problems, axis=0), 0.0)
     wide_i = jnp.where(same, jnp.concatenate([inv_i] * problems, axis=0), 0.0)
     vectors = dot_split(wide_r, sched_b) + dot_split(wide_i, turned_b)
+
+    unscaled = vectors.astype(BF16)
+    own_w[...] = unscaled
+    w_copies = []
+    for offset in range(1, groups):
+        copy = user_copy(own_w, all_w.at[me], w_send, w_recv, offset)
+        copy.start()
+        w_copies.append(copy)
+    all_w[pl.ds(me, 1)] = unscaled[None]
 
     squares = vectors * vectors
     sums = [
@@ -270,7 +346,7 @@
             dst_ref=pw_in.at[my_rb],
             send_sem=pw_send.at[offset],
             recv_sem=pw_recv.at[offset],
-            device_id={"rb": lax.rem(my_rb + offset, rb_groups)},
+            device_id={"rb": flip(my_rb, offset, rb_groups)},
             device_id_type=pl.DeviceIdType.MESH,
         )
         copy.start()
@@ -280,22 +356,23 @@
         copy.wait_recv()
     total = jnp.sum(jnp.sum(pw_in[...], axis=0), axis=1, keepdims=True)
     scale = lax.rsqrt(total / (blocks * rb_groups) + 1e-06)
-    scaled = jnp.concatenate(
+    sc_own[...] = jnp.broadcast_to(scale * scale, (8, width))
+    sc_copies = []
+    for offset in range(1, groups):
+        copy = user_copy(sc_own, sc_in.at[me], sc_send, sc_recv, offset)
+        copy.start()
+        sc_copies.append(copy)
+    sc_in[pl.ds(me, 1)] = sc_own[...][None]
+    prec = jnp.concatenate(
         [
             vectors[cell * cell_lanes : (cell + 1) * cell_lanes] * scale[cell : cell + 1, :]
             for cell in range(cell_dev)
         ],
         axis=0,
-    )
-    prec = scaled.astype(BF16)
-    own_w[...] = prec
-    w_copies = []
-    for offset in range(1, groups):
-        copy = user_copy(own_w, all_w.at[me], w_send, w_recv, offset)
-        copy.start()
-        w_copies.append(copy)
-    all_w[pl.ds(me, 1)] = prec[None]
+    ).astype(BF16)
     prec_ref[...] = prec
+    stores = [pltpu.make_async_copy(prec_ref, prec_out, store_sem.at[0])]
+    stores[0].start()
 
     prec_turned = turn(prec.astype(F32)).astype(BF16)
     z_r = dot_nt(prec, sched_b)
@@ -305,57 +382,71 @@
     signal = jnp.sum(jnp.where(on_diagonal, magnitude, 0.0), axis=0, keepdims=True)
     leakage = jnp.sum(jnp.where(on_diagonal, 0.0, magnitude), axis=0, keepdims=True)
 
-    for copy in w_copies:
+    half = groups // 2
+    near = lax.div(me, half)
+    half_cells = half * cell_dev
+    count = half_cells * beams
+    cell_shift = log2_of(half_cells)
+    new_row = iota((count, count), 0)
+    old_row = ((new_row & (half_cells - 1)) << beam_shift) + (new_row >> cell_shift)
+    order = jnp.where(old_row == iota((count, count), 1), 1.0, 0.0).astype(BF16)
+    cell_row = iota((half_cells, tracks), 0)
+    for turn_number in range(2):
+        for offset in range(1, groups):
+            if offset // half == turn_number:
+                w_copies[offset - 1].wait_recv()
+        first_group = half * (near if turn_number == 0 else 1 - near)
+        for block in range(blocks):
+            stacked = jnp.concatenate(
+                [
+                    all_w[
+                        first_group + group,
+                        cell * cell_lanes + block * beams : cell * cell_lanes + (block + 1) * beams,
+                        :,
+                    ]
+                    for group in range(half)
+                    for cell in range(cell_dev)
+                ],
+                axis=0,
+            )
+            ordered = dot_nn(order, stacked)
+            forms[block, 0:count, :] = ordered.astype(BF16)
+            forms[block, count : 2 * count, :] = turn(ordered).astype(BF16)
+
+        def track_powers(number, carry, first_cell=first_group * cell_dev, keep=turn_number):
+            slot, block = lax.div(number, blocks), lax.rem(number, blocks)
+            projected = dot_nt(forms[block], planes[number])
+            energy = jnp.sum(
+                (projected * projected).reshape(2 * beams, half_cells, tracks), axis=0
+            )
+            heard = cells_ref[slot] - first_cell
+            part = jnp.sum(jnp.where(cell_row == heard, energy, 0.0), axis=0, keepdims=True)
+            received[number] = received[number] + part if keep else part
+            return carry
+
+        lax.fori_loop(0, slots * blocks, track_powers, 0)
+
+    for copy in sc_copies:
         copy.wait_recv()
-
-    count = cells * beams
-    cell_shift = log2_of(cells)
-    new_row = iota((count, count), 0)
-    old_row = ((new_row & (cells - 1)) << beam_shift) + (new_row >> cell_shift)
-    order = jnp.where(old_row == iota((count, count), 1), 1.0, 0.0).astype(BF16)
-    for block in range(blocks):
-        stacked = jnp.concatenate(
-            [
-                all_w[
-                    group,
-                    cell * cell_lanes + block * beams : cell * cell_lanes + (block + 1) * beams,
-                    :,
-                ]
-                for group in range(groups)
-                for cell in range(cell_dev)
-            ],
-            axis=0,
-        )
-        ordered = dot_nn(order, stacked)
-        forms[block, 0:count, :] = ordered.astype(BF16)
-        forms[block, count : 2 * count, :] = turn(ordered).astype(BF16)
-
-    cell_row = iota((cells, tracks), 0)
-
-    def track_powers(number, carry):
-        slot, block = number // blocks, number % blocks
-        projected = dot_nt(forms[block], planes[number])
-        energy = jnp.sum((projected * projected).reshape(2 * beams, cells, tracks), axis=0)
+    scales = []
+    for slot in range(slots):
         heard = cells_ref[slot]
-        received[number] = jnp.sum(
-            jnp.where(cell_row == heard, energy, 0.0), axis=0, keepdims=True
-        )
-        return carry
-
-    lax.fori_loop(0, slots * blocks, track_powers, 0)
-
+        row = jnp.zeros((1, tracks), F32)
+        for group in range(groups):
+            for cell in range(cell_dev):
+                one = sc_in[group, cell : cell + 1, 0:1]
+                row = jnp.where(heard == group * cell_dev + cell, one, row)
+        scales.append(row)
     floor = jnp.zeros((1, tracks), F32)
     serving = cells_ref[0]
     for cell in range(cells):
         floor = jnp.where(serving == cell, noise_ref[cell], floor)
     denominators = []
     for block in range(blocks):
-        interference = received[blocks + block]
+        interference = received[blocks + block] * scales[1]
         for slot in range(2, slots):
-            interference = interference + received[slot * blocks + block]
+            interference = interference + received[slot * blocks + block] * scales[slot]
         denominators.append(interference + floor)
-    power = jnp.concatenate([received[block] for block in range(blocks)], axis=0)
-    all_denominators = jnp.concatenate(denominators, axis=0)
 
     found = jnp.zeros((groups * capacity, tracks), F32)
     for block in range(blocks):
@@ -379,16 +470,41 @@
         dn_copies.append(copy)
     dn_in[pl.ds(me, 1)] = dn_own[...][None]
 
+    power = jnp.concatenate([received[block] * scales[0] for block in range(blocks)], axis=0)
+    all_denominators = jnp.concatenate(denominators, axis=0)
     metric_ref[...] = jnp.log2(1.0 + power / all_denominators)
-
+    stores.append(pltpu.make_async_copy(metric_ref, metric_out, store_sem.at[1]))
+    stores[1].start()
+
+    for copy in row_copies + pw_copies + w_copies + sc_copies:
+        copy.wait_send()
     for copy in dn_copies:
         copy.wait_recv()
     every = jnp.sum(dn_in[...], axis=0)
     entry_denominator = jnp.sum(jnp.where(is_me, every, 0.0), axis=0, keepdims=True)
-    rate_ref[...] = jnp.log2(1.0 + signal / (leakage + entry_denominator))
-
-    for copy in row_copies + pw_copies + w_copies + dn_copies:
+    rate = jnp.log2(1.0 + signal / (leakage + entry_denominator))
+    for cell in range(cell_dev):
+        for block in range(blocks):
+            start = (cell * blocks + block) * beams
+            rate_ref[cell, block : block + 1, :] = rate[:, start : start + beams]
+    stores.append(pltpu.make_async_copy(rate_ref, rate_out, store_sem.at[2]))
+    stores[2].start()
+    for copy in dn_copies:
         copy.wait_send()
+    for copy in stores:
+        copy.wait()
+
+
+def hand_over(*refs):
+    count = len(refs) // 2
+    copies = [
+        pltpu.make_async_copy(refs[i], refs[count + i], refs[2 * count].at[i])
+        for i in range(count)
+    ]
+    for copy in copies:
+        copy.start()
+    for copy in copies:
+        copy.wait()
 
 
 def on_device(channel, serving, interferers, plan, regularizer, noise_floor):
@@ -400,33 +516,45 @@
     entries = cell_dev * blocks * beams
     capacity = 2 * entries // groups
     dims = (groups, rb_groups, tracks, blocks, slots, cells, beams, cell_dev, capacity)
-    rows = channel.transpose(0, 2, 1, 3).reshape(tracks * slots * blocks, width)
-    heard = jnp.concatenate([serving[None, :], interferers.T], axis=0)[:, None, :]
-    vmem = pl.BlockSpec(memory_space=pltpu.VMEM)
-    smem = pl.BlockSpec(memory_space=pltpu.SMEM)
+    row_count = tracks * slots * blocks
+    rows = channel.transpose(0, 2, 1, 3).reshape(row_count, width)
+    hbm = pl.BlockSpec(memory_space=pltpu.HBM)
     dma = pltpu.SemaphoreType.DMA
-    precoders, metric, rate = pl.pallas_call(
+    results = (
+        jax.ShapeDtypeStruct((entries, width), BF16),
+        jax.ShapeDtypeStruct((blocks, tracks), F32),
+        jax.ShapeDtypeStruct((cell_dev, blocks, beams), F32),
+    )
+    made = pl.pallas_call(
         functools.partial(kernel, dims),
-        out_shape=(
-            jax.ShapeDtypeStruct((entries, width), BF16),
-            jax.ShapeDtypeStruct((blocks, tracks), F32),
-            jax.ShapeDtypeStruct((1, entries), F32),
-        ),
-        in_specs=[vmem, vmem, vmem, smem, smem],
-        out_specs=(vmem, vmem, vmem),
+        out_shape=results,
+        in_specs=[hbm] * 6,
+        out_specs=(hbm, hbm, hbm),
         scratch_shapes=[
-            pltpu.VMEM((tracks * slots * blocks, width), F32),
+            *[pltpu.VMEM(result.shape, result.dtype) for result in results],
+            pltpu.VMEM((row_count, width), BF16),
+            pltpu.VMEM((cells, blocks, beams), jnp.int32),
+            pltpu.VMEM((slots - 1, tracks), jnp.int32),
+            pltpu.VMEM((slots, 1, tracks), jnp.int32),
+            pltpu.SMEM(regularizer.shape, F32),
+            pltpu.SMEM(noise_floor.shape, F32),
+            pltpu.VMEM((row_count, width), F32),
             pltpu.VMEM((slots * blocks, tracks, width), BF16),
             pltpu.VMEM((groups, capacity, width), BF16),
             pltpu.VMEM((groups, capacity, width), BF16),
             pltpu.VMEM((entries, width), BF16),
             pltpu.VMEM((groups, entries, width), BF16),
-            pltpu.VMEM((blocks, 2 * cells * beams, width), BF16),
+            pltpu.VMEM((blocks, cells * beams, width), BF16),
             pltpu.VMEM((slots * blocks, 1, tracks), F32),
             pltpu.VMEM((8, width), F32),
             pltpu.VMEM((rb_groups, 8, width), F32),
+            pltpu.VMEM((8, width), F32),
+            pltpu.VMEM((groups, 8, width), F32),
             pltpu.VMEM((groups, entries), F32),
             pltpu.VMEM((groups, groups, entries), F32),
+            dma((8,)),
+            dma((5,)),
+            dma((3,)),
             dma((groups,)),
             dma((groups,)),
             dma((groups,)),
@@ -435,16 +563,22 @@
             dma((rb_groups,)),
             dma((groups,)),
             dma((groups,)),
+            dma((groups,)),
+            dma((groups,)),
         ],
         compiler_params=pltpu.CompilerParams(
-            collective_id=0, has_side_effects=True, vmem_limit_bytes=48 << 20
+            collective_id=0, has_side_effects=True, vmem_limit_bytes=64 << 20
         ),
-    )(rows, plan.reshape(groups, entries), heard, regularizer, noise_floor)
-    return (
-        precoders.reshape(cell_dev, blocks, beams, width),
-        metric.T,
-        rate.reshape(cell_dev, blocks, beams),
-    )
+    )(rows, plan, serving[None, :], interferers.T, regularizer, noise_floor)
+    precoders, metric, rate = pl.pallas_call(
+        hand_over,
+        out_shape=results,
+        in_specs=[hbm] * 3,
+        out_specs=(hbm, hbm, hbm),
+        scratch_shapes=[dma((3,))],
+        compiler_params=pltpu.CompilerParams(vmem_limit_bytes=64 << 20),
+    )(*made)
+    return precoders.reshape(cell_dev, blocks, beams, width), metric.T, rate
 
 
 def solution(mesh):

time: 43.9 us -> 35.3 us (0.80)
  local copies, waits for them, and re-layouts: 6.47 us -> 0 us
  other arithmetic: 1.38 us -> 0 us
  Pallas kernels: 35.1 us -> 34.5 us
    unnamed x8 -> x0, local copies, waits for them, and re-layouts: 4.41 us -> none
    reshape x2 -> x0, local copies, waits for them, and re-layouts: 1.53 us -> none  [the longest x1 0.84 us: on_device(): plan.reshape(groups, entries)]
    concatenate x1 -> x0, other arithmetic: 0.71 us -> none  [on_device(): jnp.concatenate([serving[None, :], interferers.T], axis=0)[:, None, :]]
    pallas_call x1 -> x0, other arithmetic: 0.66 us -> none  [on_device(): pl.pallas_call(functools.partial(kernel, dims), out_shape=(jax.ShapeDtype...]
    pallas_call x1 -> x2, Pallas kernels: 35.1 us -> 34.5 us  [the longest x1 31.8 us: on_device(): pl.pallas_call(functools.partial(kernel, dims), out_shape=results, in_spe...]
    pallas_call x1 -> x0, local copies, waits for them, and re-layouts: 0.51 us -> none  [on_device(): pl.pallas_call(functools.partial(kernel, dims), out_shape=(jax.ShapeDtype...]
where the time goes in v2:
time: 35.3 us; the launch traced here: 35.2 us
  Pallas kernels  34.5 us (98%)
  between operations  0.64 us (2%)
    pallas_call x1, Pallas kernels, on_device(): pl.pallas_call(functools.partial(kernel, dims), out_shape=results, in_spe...  31.8 us
    pallas_call x1, Pallas kernels, on_device(): pl.pallas_call(hand_over, out_shape=results, in_specs=[hbm] * 3, out_spec...  2.74 us

profile of v2, /device:TPU:0, one launch (start us, length us, event | category | flops | bytes accessed | tf_op | source)
XLA Modules:
  0.0 35.2 jit_solution(16809556961060161781)
XLA Ops:
  0.6 31.8 %shard_map.85 = (bf16[128,128]{1,0:T(8,128)(2,1)}, f32[4,1024]{1,0:T(4,128)}, f32[2,4,16]{2,1,0:T(4,128)}) custom-call(bf16[12288,128]{1,0:T(8,128)(2,1)} %bitcast.7, s32[16,4,16]{2,1,0:T(4,128)} %plan_hbm.1, s32[1,1024]{1,0:T(1,128)} %bitcast.9, s32[2,1024]{1,0:T(2,128)} %bitcast.8, f32[2]{0:T(128)} %reg_hbm.1, f32[16]{0:T(128)} %noise_hbm.1), custom_call_target="tpu_custom_call" | custom-call | tf_op jit(solution)/shard_map/pallas_call | solution.py:528
  32.4 2.7 %shard_map.86 = (bf16[128,128]{1,0:T(8,128)(2,1)}, f32[4,1024]{1,0:T(4,128)}, f32[2,4,16]{2,1,0:T(4,128)}) custom-call(bf16[128,128]{1,0:T(8,128)(2,1)} %get-tuple-element.9.refs_0_, f32[4,1024]{1,0:T(4,128)} %get-tuple-element.10.refs_1_, f32[2,4,16]{2,1,0:T(4,128)} %get-tuple-element.11.refs_2_), custom_call_target="tpu_custom_call" | custom-call | tf_op jit(solution)/shard_map/pallas_call | solution.py:573

commit v3 on v2

--- a/solution.py
+++ b/solution.py
@@ -80,8 +80,9 @@
         precision=HIGH,
         preferred_element_type=F32,
     )[0:1, :]
-    start_r = jnp.where(diagonal, 1.0 / trace, 0.0)
-    start_i = jnp.zeros(shape, F32)
+    first = 1.0 / trace
+    start_r = jnp.where(diagonal, 2.0 * first, 0.0) - gram_r * first * first
+    start_i = -(gram_i * first * first)
     gather_r, gather_i = spread(gram_r, beams), spread(gram_i, beams)
     held_r = [gather_r(m) for m in range(beams)]
     held_i = [gather_i(m) for m in range(beams)]
@@ -92,7 +93,7 @@
         zr, zi = complex_product(spread(xr, beams), spread(xi, beams), yr, yi, beams)
         return 2.0 * xr - zr, 2.0 * xi - zi
 
-    return lax.fori_loop(0, ITERS, step, (start_r, start_i))
+    return lax.fori_loop(1, ITERS, step, (start_r, start_i))
 
 
 def flip(index, mask, count):
@@ -113,9 +114,6 @@
     inter_hbm,
     reg_hbm,
     noise_hbm,
-    prec_out,
-    metric_out,
-    rate_out,
     prec_ref,
     metric_ref,
     rate_ref,
@@ -129,6 +127,10 @@
     planes,
     out_rows,
     in_rows,
+    out_more,
+    in_more,
+    out_ids,
+    in_ids,
     own_w,
     all_w,
     forms,
@@ -137,21 +139,20 @@
     pw_in,
     sc_own,
     sc_in,
-    dn_own,
-    dn_in,
     load_sem,
     small_sem,
-    store_sem,
     row_send,
     row_recv,
+    more_send,
+    more_recv,
+    ids_send,
+    ids_recv,
     w_send,
     w_recv,
     pw_send,
     pw_recv,
     sc_send,
     sc_recv,
-    dn_send,
-    dn_recv,
 ):
     groups, rb_groups, tracks, blocks, slots, cells, beams, cell_dev, capacity = dims
     entries = cell_dev * blocks * beams
@@ -266,9 +267,10 @@
 
     track_lane = iota((groups * capacity, tracks), 1)
     gathered = None
+    hots = []
     for block in range(blocks):
-        one_hot = jnp.where(picks - block * tracks == track_lane, 1.0, 0.0).astype(BF16)
-        part = dot_nn(one_hot, planes[block])
+        hots.append(jnp.where(picks - block * tracks == track_lane, 1.0, 0.0).astype(BF16))
+        part = dot_nn(hots[block], planes[block])
         gathered = part if gathered is None else gathered + part
     for group in range(groups):
         out_rows[group] = gathered[group * capacity : (group + 1) * capacity].astype(BF16)
@@ -286,14 +288,38 @@
     for slot in range(1, slots):
         extract(slot)
 
+    gathered = any_hot = None
+    for block in range(blocks):
+        planes_of = [planes[slot * blocks + block] for slot in range(1, slots)]
+        part = dot_nn(hots[block], jnp.concatenate(planes_of, axis=1))
+        gathered = part if gathered is None else gathered + part
+        any_hot = hots[block] if any_hot is None else any_hot + hots[block]
+    heard_rows = [cells_ref[slot].astype(F32) for slot in range(1, slots)]
+    heard_rows.append(jnp.zeros((9 - slots, tracks), F32))
+    ids = dot_nt(jnp.concatenate(heard_rows, axis=0).astype(BF16), any_hot)
+    out_ids[...] = jnp.zeros(out_ids.shape, F32)
+    for group in range(groups):
+        part = slice(group * capacity, (group + 1) * capacity)
+        out_more[group] = gathered[part].astype(BF16)
+        out_ids[group, :, 0:capacity] = ids[:, part]
+    more_copies = []
+    for offset in range(1, groups):
+        dst = flip(me, offset, groups)
+        copy = user_copy(out_more.at[dst], in_more.at[me], more_send, more_recv, offset)
+        copy.start()
+        more_copies.append(copy)
+        copy = user_copy(out_ids.at[dst], in_ids.at[me], ids_send, ids_recv, offset)
+        copy.start()
+        more_copies.append(copy)
+    in_more[pl.ds(me, 1)] = out_more[pl.ds(me, 1)]
+    in_ids[pl.ds(me, 1)] = out_ids[pl.ds(me, 1)]
+
     is_me = iota(ent.shape, 0) == me
     my_owner = jnp.sum(jnp.where(is_me, owner.astype(F32), 0.0), axis=0, keepdims=True)
     from_src = jnp.where(my_owner == iota(ent.shape, 0).astype(F32), 1.0, 0.0)
     src_rank = dot_nn(from_src.astype(BF16), before)
-    arrivals = jnp.concatenate(
-        [hits_of(from_src, src_rank, group) for group in range(groups)], axis=0
-    )
-    place = jnp.transpose(arrivals).astype(BF16)
+    arrivals = [hits_of(from_src, src_rank, group) for group in range(groups)]
+    place = jnp.transpose(jnp.concatenate(arrivals, axis=0)).astype(BF16)
 
     for copy in row_copies:
         copy.wait_recv()
@@ -324,7 +350,11 @@
     wide_i = jnp.where(same, jnp.concatenate([inv_i] * problems, axis=0), 0.0)
     vectors = dot_split(wide_r, sched_b) + dot_split(wide_i, turned_b)
 
-    unscaled = vectors.astype(BF16)
+    cell_shift = log2_of(cell_dev)
+    new_row = iota(square, 0)
+    old_row = (new_row & (cell_dev - 1)) * cell_lanes + (new_row >> cell_shift)
+    order = jnp.where(old_row == iota(square, 1), 1.0, 0.0).astype(BF16)
+    unscaled = dot_nn(order, vectors.astype(BF16)).astype(BF16)
     own_w[...] = unscaled
     w_copies = []
     for offset in range(1, groups):
@@ -371,8 +401,6 @@
         axis=0,
     ).astype(BF16)
     prec_ref[...] = prec
-    stores = [pltpu.make_async_copy(prec_ref, prec_out, store_sem.at[0])]
-    stores[0].start()
 
     prec_turned = turn(prec.astype(F32)).astype(BF16)
     z_r = dot_nt(prec, sched_b)
@@ -382,117 +410,109 @@
     signal = jnp.sum(jnp.where(on_diagonal, magnitude, 0.0), axis=0, keepdims=True)
     leakage = jnp.sum(jnp.where(on_diagonal, 0.0, magnitude), axis=0, keepdims=True)
 
+    for copy in more_copies:
+        copy.wait_recv()
+    came = jnp.concatenate([in_more[group].astype(F32) for group in range(groups)], axis=0)
+    more = dot_nn(place, came.astype(BF16))
+    entry_rows = jnp.concatenate(
+        [more[:, slot * width : (slot + 1) * width] for slot in range(slots - 1)], axis=0
+    ).astype(BF16)
+    entry_ids = jnp.zeros((8, entries), F32)
+    for group in range(groups):
+        known = in_ids[group, :, 0:capacity].astype(BF16)
+        entry_ids = entry_ids + dot_nn(known, arrivals[group].astype(BF16))
+    entry_heard = jnp.concatenate(
+        [entry_ids[slot : slot + 1, :] for slot in range(slots - 1)], axis=1
+    ).astype(jnp.int32)
+    entry_lanes = (slots - 1) * entries
+    entry_block = (iota((1, entry_lanes), 1) >> beam_shift) & (blocks - 1)
+
     half = groups // 2
     near = lax.div(me, half)
-    half_cells = half * cell_dev
-    count = half_cells * beams
-    cell_shift = log2_of(half_cells)
-    new_row = iota((count, count), 0)
-    old_row = ((new_row & (half_cells - 1)) << beam_shift) + (new_row >> cell_shift)
-    order = jnp.where(old_row == iota((count, count), 1), 1.0, 0.0).astype(BF16)
-    cell_row = iota((half_cells, tracks), 0)
+    part_rows = cell_dev * beams
+    form_rows = 2 * part_rows
+
+    def heard_power(form, rows, heard):
+        lanes = rows.shape[0]
+        projected = dot_nt(form, rows)
+        energy = jnp.sum(
+            (projected * projected).reshape(half, form_rows // 8, 8, lanes), axis=1
+        )
+        shape = (half, 8, lanes)
+        cell = iota(shape, 0) * cell_dev + (iota(shape, 1) & (cell_dev - 1))
+        found = jnp.sum(jnp.where(cell == heard[None], energy, 0.0), axis=0)
+        return jnp.sum(found, axis=0, keepdims=True)
+
+    entry_power = jnp.zeros((1, entry_lanes), F32)
     for turn_number in range(2):
         for offset in range(1, groups):
             if offset // half == turn_number:
                 w_copies[offset - 1].wait_recv()
         first_group = half * (near if turn_number == 0 else 1 - near)
+        first_cell = first_group * cell_dev
         for block in range(blocks):
-            stacked = jnp.concatenate(
-                [
-                    all_w[
-                        first_group + group,
-                        cell * cell_lanes + block * beams : cell * cell_lanes + (block + 1) * beams,
-                        :,
-                    ]
-                    for group in range(half)
-                    for cell in range(cell_dev)
-                ],
-                axis=0,
-            )
-            ordered = dot_nn(order, stacked)
-            forms[block, 0:count, :] = ordered.astype(BF16)
-            forms[block, count : 2 * count, :] = turn(ordered).astype(BF16)
-
-        def track_powers(number, carry, first_cell=first_group * cell_dev, keep=turn_number):
-            slot, block = lax.div(number, blocks), lax.rem(number, blocks)
-            projected = dot_nt(forms[block], planes[number])
-            energy = jnp.sum(
-                (projected * projected).reshape(2 * beams, half_cells, tracks), axis=0
-            )
+            for group in range(half):
+                rows_in = all_w[first_group + group, block * part_rows : (block + 1) * part_rows, :]
+                at = group * form_rows
+                forms[block, at : at + part_rows, :] = rows_in
+                forms[block, at + part_rows : at + form_rows, :] = turn(
+                    rows_in.astype(F32)
+                ).astype(BF16)
+
+        def track_powers(slot, carry, first_cell=first_cell, keep=turn_number):
             heard = cells_ref[slot] - first_cell
-            part = jnp.sum(jnp.where(cell_row == heard, energy, 0.0), axis=0, keepdims=True)
-            received[number] = received[number] + part if keep else part
+            for block in range(blocks):
+                number = slot * blocks + block
+                part = heard_power(forms[block], planes[number], heard)
+                received[number] = received[number] + part if keep else part
             return carry
 
-        lax.fori_loop(0, slots * blocks, track_powers, 0)
+        lax.fori_loop(0, slots, track_powers, 0)
+        for block in range(blocks):
+            part = heard_power(forms[block], entry_rows, entry_heard - first_cell)
+            entry_power = entry_power + jnp.where(entry_block == block, part, 0.0)
 
     for copy in sc_copies:
         copy.wait_recv()
-    scales = []
-    for slot in range(slots):
-        heard = cells_ref[slot]
-        row = jnp.zeros((1, tracks), F32)
+
+    def scale_row(heard):
+        row = jnp.zeros(heard.shape, F32)
         for group in range(groups):
             for cell in range(cell_dev):
                 one = sc_in[group, cell : cell + 1, 0:1]
                 row = jnp.where(heard == group * cell_dev + cell, one, row)
-        scales.append(row)
-    floor = jnp.zeros((1, tracks), F32)
-    serving = cells_ref[0]
-    for cell in range(cells):
-        floor = jnp.where(serving == cell, noise_ref[cell], floor)
-    denominators = []
-    for block in range(blocks):
-        interference = received[blocks + block] * scales[1]
-        for slot in range(2, slots):
-            interference = interference + received[slot * blocks + block] * scales[slot]
-        denominators.append(interference + floor)
-
-    found = jnp.zeros((groups * capacity, tracks), F32)
-    for block in range(blocks):
-        found = jnp.where(picks - block * tracks == track_lane, denominators[block], found)
-    column = jnp.sum(found, axis=1, keepdims=True)
-    dn_own[...] = jnp.concatenate(
-        [
-            jnp.sum(
-                sends[group] * column[group * capacity : (group + 1) * capacity],
-                axis=0,
-                keepdims=True,
-            )
-            for group in range(groups)
-        ],
-        axis=0,
-    )
-    dn_copies = []
-    for offset in range(1, groups):
-        copy = user_copy(dn_own, dn_in.at[me], dn_send, dn_recv, offset)
-        copy.start()
-        dn_copies.append(copy)
-    dn_in[pl.ds(me, 1)] = dn_own[...][None]
-
-    power = jnp.concatenate([received[block] * scales[0] for block in range(blocks)], axis=0)
-    all_denominators = jnp.concatenate(denominators, axis=0)
-    metric_ref[...] = jnp.log2(1.0 + power / all_denominators)
-    stores.append(pltpu.make_async_copy(metric_ref, metric_out, store_sem.at[1]))
-    stores[1].start()
-
-    for copy in row_copies + pw_copies + w_copies + sc_copies:
-        copy.wait_send()
-    for copy in dn_copies:
-        copy.wait_recv()
-    every = jnp.sum(dn_in[...], axis=0)
-    entry_denominator = jnp.sum(jnp.where(is_me, every, 0.0), axis=0, keepdims=True)
+        return row
+
+    entry_power = entry_power * scale_row(entry_heard)
+    entry_denominator = entry_power[:, 0:entries]
+    for slot in range(1, slots - 1):
+        entry_denominator = entry_denominator + entry_power[:, slot * entries : (slot + 1) * entries]
+    noise_lanes = jnp.zeros((1, entries), F32)
+    for cell in range(cell_dev):
+        noise_lanes = jnp.where(
+            lane_e >= cell * cell_lanes, noise_ref[me * cell_dev + cell], noise_lanes
+        )
+    entry_denominator = entry_denominator + noise_lanes
     rate = jnp.log2(1.0 + signal / (leakage + entry_denominator))
     for cell in range(cell_dev):
         for block in range(blocks):
             start = (cell * blocks + block) * beams
             rate_ref[cell, block : block + 1, :] = rate[:, start : start + beams]
-    stores.append(pltpu.make_async_copy(rate_ref, rate_out, store_sem.at[2]))
-    stores[2].start()
-    for copy in dn_copies:
+
+    scales = [scale_row(cells_ref[slot]) for slot in range(slots)]
+    floor = jnp.zeros((1, tracks), F32)
+    serving = cells_ref[0]
+    for cell in range(cells):
+        floor = jnp.where(serving == cell, noise_ref[cell], floor)
+    for block in range(blocks):
+        interference = received[blocks + block] * scales[1]
+        for slot in range(2, slots):
+            interference = interference + received[slot * blocks + block] * scales[slot]
+        power = received[block] * scales[0]
+        metric_ref[block : block + 1, :] = jnp.log2(1.0 + power / (interference + floor))
+
+    for copy in row_copies + more_copies + pw_copies + w_copies + sc_copies:
         copy.wait_send()
-    for copy in stores:
-        copy.wait()
 
 
 def hand_over(*refs):
@@ -519,6 +539,7 @@
     row_count = tracks * slots * blocks
     rows = channel.transpose(0, 2, 1, 3).reshape(row_count, width)
     hbm = pl.BlockSpec(memory_space=pltpu.HBM)
+    vmem = pl.BlockSpec(memory_space=pltpu.VMEM)
     dma = pltpu.SemaphoreType.DMA
     results = (
         jax.ShapeDtypeStruct((entries, width), BF16),
@@ -529,9 +550,8 @@
         functools.partial(kernel, dims),
         out_shape=results,
         in_specs=[hbm] * 6,
-        out_specs=(hbm, hbm, hbm),
+        out_specs=(vmem, vmem, vmem),
         scratch_shapes=[
-            *[pltpu.VMEM(result.shape, result.dtype) for result in results],
             pltpu.VMEM((row_count, width), BF16),
             pltpu.VMEM((cells, blocks, beams), jnp.int32),
             pltpu.VMEM((slots - 1, tracks), jnp.int32),
@@ -542,6 +562,10 @@
             pltpu.VMEM((slots * blocks, tracks, width), BF16),
             pltpu.VMEM((groups, capacity, width), BF16),
             pltpu.VMEM((groups, capacity, width), BF16),
+            pltpu.VMEM((groups, capacity, (slots - 1) * width), BF16),
+            pltpu.VMEM((groups, capacity, (slots - 1) * width), BF16),
+            pltpu.VMEM((groups, 8, width), F32),
+            pltpu.VMEM((groups, 8, width), F32),
             pltpu.VMEM((entries, width), BF16),
             pltpu.VMEM((groups, entries, width), BF16),
             pltpu.VMEM((blocks, cells * beams, width), BF16),
@@ -550,19 +574,11 @@
             pltpu.VMEM((rb_groups, 8, width), F32),
             pltpu.VMEM((8, width), F32),
             pltpu.VMEM((groups, 8, width), F32),
-            pltpu.VMEM((groups, entries), F32),
-            pltpu.VMEM((groups, groups, entries), F32),
             dma((8,)),
             dma((5,)),
-            dma((3,)),
-            dma((groups,)),
-            dma((groups,)),
-            dma((groups,)),
-            dma((groups,)),
+            *[dma((groups,)) for _ in range(8)],
             dma((rb_groups,)),
             dma((rb_groups,)),
-            dma((groups,)),
-            dma((groups,)),
             dma((groups,)),
             dma((groups,)),
         ],
@@ -573,7 +589,7 @@
     precoders, metric, rate = pl.pallas_call(
         hand_over,
         out_shape=results,
-        in_specs=[hbm] * 3,
+        in_specs=[vmem] * 3,
         out_specs=(hbm, hbm, hbm),
         scratch_shapes=[dma((3,))],
         compiler_params=pltpu.CompilerParams(vmem_limit_bytes=64 << 20),

time: 35.3 us -> 28 us (0.79)
  Pallas kernels: 34.5 us -> 27.1 us
    pallas_call x1, Pallas kernels: 31.8 us -> 25.7 us  [on_device(): pl.pallas_call(functools.partial(kernel, dims), out_shape=results, in_spe...]
    pallas_call x1, Pallas kernels: 2.74 us -> 1.42 us  [on_device(): pl.pallas_call(hand_over, out_shape=results, in_specs=[vmem] * 3, out_spe...]
where the time goes in v3:
time: 28 us; the launch traced here: 27.8 us
  Pallas kernels  27.1 us (97%)
  between operations  0.64 us (2%)
    pallas_call x1, Pallas kernels, on_device(): pl.pallas_call(functools.partial(kernel, dims), out_shape=results, in_spe...  25.7 us
    pallas_call x1, Pallas kernels, on_device(): pl.pallas_call(hand_over, out_shape=results, in_specs=[vmem] * 3, out_spe...  1.42 us

profile of v3, /device:TPU:0, one launch (start us, length us, event | category | flops | bytes accessed | tf_op | source)
XLA Modules:
  0.0 27.8 jit_solution(2334578145778109653)
XLA Ops:
  0.6 25.7 %shard_map.85 = (bf16[128,128]{1,0:T(8,128)(2,1)}, f32[4,1024]{1,0:T(4,128)}, f32[2,4,16]{2,1,0:T(4,128)}) custom-call(bf16[12288,128]{1,0:T(8,128)(2,1)} %bitcast.7, s32[16,4,16]{2,1,0:T(4,128)} %plan_hbm.1, s32[1,1024]{1,0:T(1,128)} %bitcast.9, s32[2,1024]{1,0:T(2,128)} %bitcast.8, f32[2]{0:T(128)} %reg_hbm.1, f32[16]{0:T(128)} %noise_hbm.1), custom_call_target="tpu_custom_call" | custom-call | tf_op jit(solution)/shard_map/pallas_call | solution.py:549
  26.3 1.4 %shard_map.86 = (bf16[128,128]{1,0:T(8,128)(2,1)}, f32[4,1024]{1,0:T(4,128)}, f32[2,4,16]{2,1,0:T(4,128)}) custom-call(bf16[128,128]{1,0:T(8,128)(2,1)} %get-tuple-element.9.refs_0_, f32[4,1024]{1,0:T(4,128)} %get-tuple-element.10.refs_1_, f32[2,4,16]{2,1,0:T(4,128)} %get-tuple-element.11.refs_2_), custom_call_target="tpu_custom_call" | custom-call | tf_op jit(solution)/shard_map/pallas_call | solution.py:589

commit v4 on v3

--- a/solution.py
+++ b/solution.py
@@ -36,16 +36,10 @@
     return jnp.dot(a, b, preferred_element_type=F32)
 
 
-def split3(x):
+def dot_split(x, b):
     high = x.astype(BF16)
-    rest = x - high.astype(F32)
-    middle = rest.astype(BF16)
-    return high, middle, (rest - middle.astype(F32)).astype(BF16)
-
-
-def dot_split(x, b):
-    high, middle, low = split3(x)
-    return dot_nn(low, b) + dot_nn(middle, b) + dot_nn(high, b)
+    rest = (x - high.astype(F32)).astype(BF16)
+    return dot_nn(rest, b) + dot_nn(high, b)
 
 
 def spread(a, beams):
@@ -81,19 +75,28 @@
         preferred_element_type=F32,
     )[0:1, :]
     first = 1.0 / trace
-    start_r = jnp.where(diagonal, 2.0 * first, 0.0) - gram_r * first * first
-    start_i = -(gram_i * first * first)
-    gather_r, gather_i = spread(gram_r, beams), spread(gram_i, beams)
-    held_r = [gather_r(m) for m in range(beams)]
-    held_i = [gather_i(m) for m in range(beams)]
+    rest_r = jnp.where(diagonal, 1.0, 0.0) - gram_r * first
+    rest_i = -(gram_i * first)
+    start_r = jnp.where(diagonal, first, 0.0) + rest_r * first
+    start_i = rest_i * first
+
+    def square_of(rr, ri):
+        return complex_product(spread(rr, beams), spread(ri, beams), rr, ri, beams)
 
     def step(_, carry):
-        xr, xi = carry
-        yr, yi = complex_product(lambda m: held_r[m], lambda m: held_i[m], xr, xi, beams)
-        zr, zi = complex_product(spread(xr, beams), spread(xi, beams), yr, yi, beams)
-        return 2.0 * xr - zr, 2.0 * xi - zi
-
-    return lax.fori_loop(1, ITERS, step, (start_r, start_i))
+        rr, ri, xr, xi = carry
+        left_r, left_i = spread(rr, beams), spread(ri, beams)
+        both_r = jnp.concatenate([xr, rr], axis=1)
+        both_i = jnp.concatenate([xi, ri], axis=1)
+        twice_r = lambda m: jnp.concatenate([left_r(m)] * 2, axis=1)
+        twice_i = lambda m: jnp.concatenate([left_i(m)] * 2, axis=1)
+        zr, zi = complex_product(twice_r, twice_i, both_r, both_i, beams)
+        return zr[:, lanes:], zi[:, lanes:], xr + zr[:, :lanes], xi + zi[:, :lanes]
+
+    one_r, one_i = square_of(rest_r, rest_i)
+    rr, ri, xr, xi = lax.fori_loop(1, ITERS - 1, step, (one_r, one_i, start_r, start_i))
+    zr, zi = complex_product(spread(rr, beams), spread(ri, beams), xr, xi, beams)
+    return xr + zr, xi + zi
 
 
 def flip(index, mask, count):
@@ -301,7 +304,7 @@
     for group in range(groups):
         part = slice(group * capacity, (group + 1) * capacity)
         out_more[group] = gathered[part].astype(BF16)
-        out_ids[group, :, 0:capacity] = ids[:, part]
+        out_ids[group, :, 0:capacity] = ids[0 : slots - 1, part]
     more_copies = []
     for offset in range(1, groups):
         dst = flip(me, offset, groups)
@@ -348,7 +351,10 @@
     same = (iota(square, 0) >> beam_shift) == (iota(square, 1) >> beam_shift)
     wide_r = jnp.where(same, jnp.concatenate([inv_r] * problems, axis=0), 0.0)
     wide_i = jnp.where(same, jnp.concatenate([inv_i] * problems, axis=0), 0.0)
-    vectors = dot_split(wide_r, sched_b) + dot_split(wide_i, turned_b)
+    vectors = dot_split(
+        jnp.concatenate([wide_r, wide_i], axis=1),
+        jnp.concatenate([sched_b, turned_b], axis=0),
+    )
 
     cell_shift = log2_of(cell_dev)
     new_row = iota(square, 0)
@@ -417,7 +423,7 @@
     entry_rows = jnp.concatenate(
         [more[:, slot * width : (slot + 1) * width] for slot in range(slots - 1)], axis=0
     ).astype(BF16)
-    entry_ids = jnp.zeros((8, entries), F32)
+    entry_ids = jnp.zeros((slots - 1, entries), F32)
     for group in range(groups):
         known = in_ids[group, :, 0:capacity].astype(BF16)
         entry_ids = entry_ids + dot_nn(known, arrivals[group].astype(BF16))
@@ -564,8 +570,8 @@
             pltpu.VMEM((groups, capacity, width), BF16),
             pltpu.VMEM((groups, capacity, (slots - 1) * width), BF16),
             pltpu.VMEM((groups, capacity, (slots - 1) * width), BF16),
-            pltpu.VMEM((groups, 8, width), F32),
-            pltpu.VMEM((groups, 8, width), F32),
+            pltpu.VMEM((groups, slots - 1, width), F32),
+            pltpu.VMEM((groups, slots - 1, width), F32),
             pltpu.VMEM((entries, width), BF16),
             pltpu.VMEM((groups, entries, width), BF16),
             pltpu.VMEM((blocks, cells * beams, width), BF16),

time: 28 us -> 28.1 us (level)
  no operation moved by 1% of the time
where the time goes in v4:
time: 28.1 us; the launch traced here: 27.9 us
  Pallas kernels  27.3 us (97%)
  between operations  0.64 us (2%)
    pallas_call x1, Pallas kernels, on_device(): pl.pallas_call(functools.partial(kernel, dims), out_shape=results, in_spe...  25.8 us
    pallas_call x1, Pallas kernels, on_device(): pl.pallas_call(hand_over, out_shape=results, in_specs=[vmem] * 3, out_spe...  1.42 us

profile of v4, /device:TPU:0, one launch (start us, length us, event | category | flops | bytes accessed | tf_op | source)
XLA Modules:
  0.0 27.9 jit_solution(117166573861576429)
XLA Ops:
  0.6 25.8 %shard_map.85 = (bf16[128,128]{1,0:T(8,128)(2,1)}, f32[4,1024]{1,0:T(4,128)}, f32[2,4,16]{2,1,0:T(4,128)}) custom-call(bf16[12288,128]{1,0:T(8,128)(2,1)} %bitcast.7, s32[16,4,16]{2,1,0:T(4,128)} %plan_hbm.1, s32[1,1024]{1,0:T(1,128)} %bitcast.9, s32[2,1024]{1,0:T(2,128)} %bitcast.8, f32[2]{0:T(128)} %reg_hbm.1, f32[16]{0:T(128)} %noise_hbm.1), custom_call_target="tpu_custom_call" | custom-call | tf_op jit(solution)/shard_map/pallas_call | solution.py:555
  26.5 1.4 %shard_map.86 = (bf16[128,128]{1,0:T(8,128)(2,1)}, f32[4,1024]{1,0:T(4,128)}, f32[2,4,16]{2,1,0:T(4,128)}) custom-call(bf16[128,128]{1,0:T(8,128)(2,1)} %get-tuple-element.9.refs_0_, f32[4,1024]{1,0:T(4,128)} %get-tuple-element.10.refs_1_, f32[2,4,16]{2,1,0:T(4,128)} %get-tuple-element.11.refs_2_), custom_call_target="tpu_custom_call" | custom-call | tf_op jit(solution)/shard_map/pallas_call | solution.py:595

commit v5 on v3

--- a/solution.py
+++ b/solution.py
@@ -301,7 +301,7 @@
     for group in range(groups):
         part = slice(group * capacity, (group + 1) * capacity)
         out_more[group] = gathered[part].astype(BF16)
-        out_ids[group, :, 0:capacity] = ids[:, part]
+        out_ids[group, :, 0:capacity] = ids[0 : slots - 1, part]
     more_copies = []
     for offset in range(1, groups):
         dst = flip(me, offset, groups)
@@ -356,11 +356,12 @@
     order = jnp.where(old_row == iota(square, 1), 1.0, 0.0).astype(BF16)
     unscaled = dot_nn(order, vectors.astype(BF16)).astype(BF16)
     own_w[...] = unscaled
-    w_copies = []
+    half = groups // 2
+    w_copies = {}
     for offset in range(1, groups):
-        copy = user_copy(own_w, all_w.at[me], w_send, w_recv, offset)
-        copy.start()
-        w_copies.append(copy)
+        if offset < half or offset % 2 == 0:
+            w_copies[offset] = user_copy(own_w, all_w.at[me], w_send, w_recv, offset)
+            w_copies[offset].start()
     all_w[pl.ds(me, 1)] = unscaled[None]
 
     squares = vectors * vectors
@@ -417,7 +418,7 @@
     entry_rows = jnp.concatenate(
         [more[:, slot * width : (slot + 1) * width] for slot in range(slots - 1)], axis=0
     ).astype(BF16)
-    entry_ids = jnp.zeros((8, entries), F32)
+    entry_ids = jnp.zeros((slots - 1, entries), F32)
     for group in range(groups):
         known = in_ids[group, :, 0:capacity].astype(BF16)
         entry_ids = entry_ids + dot_nn(known, arrivals[group].astype(BF16))
@@ -427,50 +428,79 @@
     entry_lanes = (slots - 1) * entries
     entry_block = (iota((1, entry_lanes), 1) >> beam_shift) & (blocks - 1)
 
-    half = groups // 2
     near = lax.div(me, half)
+    parity = lax.rem(me, 2)
     part_rows = cell_dev * beams
     form_rows = 2 * part_rows
 
-    def heard_power(form, rows, heard):
+    def heard_power(form, rows, heard, count, step):
         lanes = rows.shape[0]
         projected = dot_nt(form, rows)
         energy = jnp.sum(
-            (projected * projected).reshape(half, form_rows // 8, 8, lanes), axis=1
-        )
-        shape = (half, 8, lanes)
-        cell = iota(shape, 0) * cell_dev + (iota(shape, 1) & (cell_dev - 1))
+            (projected * projected).reshape(count, form_rows // 8, 8, lanes), axis=1
+        )
+        shape = (count, 8, lanes)
+        cell = iota(shape, 0) * (step * cell_dev) + (iota(shape, 1) & (cell_dev - 1))
         found = jnp.sum(jnp.where(cell == heard[None], energy, 0.0), axis=0)
         return jnp.sum(found, axis=0, keepdims=True)
 
-    entry_power = jnp.zeros((1, entry_lanes), F32)
-    for turn_number in range(2):
-        for offset in range(1, groups):
-            if offset // half == turn_number:
-                w_copies[offset - 1].wait_recv()
-        first_group = half * (near if turn_number == 0 else 1 - near)
+    def hand_on():
+        for offset in range(half, groups, 2):
+            w_copies[offset].wait_recv()
+            source = flip(me, offset, groups)
+            relay = pltpu.make_async_remote_copy(
+                src_ref=all_w.at[source],
+                dst_ref=all_w.at[source],
+                send_sem=w_send.at[offset + 1],
+                recv_sem=w_recv.at[offset + 1],
+                device_id={"users": flip(me, 1, groups)},
+                device_id_type=pl.DeviceIdType.MESH,
+            )
+            relay.start()
+            w_copies[offset + 1] = relay
+
+    def add_powers(first_group, count, step, keep, middle):
         first_cell = first_group * cell_dev
+        size = count * form_rows
         for block in range(blocks):
-            for group in range(half):
-                rows_in = all_w[first_group + group, block * part_rows : (block + 1) * part_rows, :]
-                at = group * form_rows
+            for number in range(count):
+                rows_in = all_w[
+                    first_group + step * number, block * part_rows : (block + 1) * part_rows, :
+                ]
+                at = number * form_rows
                 forms[block, at : at + part_rows, :] = rows_in
                 forms[block, at + part_rows : at + form_rows, :] = turn(
                     rows_in.astype(F32)
                 ).astype(BF16)
 
-        def track_powers(slot, carry, first_cell=first_cell, keep=turn_number):
+        def track_powers(slot, carry):
             heard = cells_ref[slot] - first_cell
             for block in range(blocks):
                 number = slot * blocks + block
-                part = heard_power(forms[block], planes[number], heard)
+                part = heard_power(forms[block, 0:size], planes[number], heard, count, step)
                 received[number] = received[number] + part if keep else part
             return carry
 
-        lax.fori_loop(0, slots, track_powers, 0)
+        if middle is None:
+            lax.fori_loop(0, slots, track_powers, 0)
+        else:
+            lax.fori_loop(0, slots - 1, track_powers, 0)
+            middle()
+            track_powers(slots - 1, 0)
+        total = jnp.zeros((1, entry_lanes), F32)
         for block in range(blocks):
-            part = heard_power(forms[block], entry_rows, entry_heard - first_cell)
-            entry_power = entry_power + jnp.where(entry_block == block, part, 0.0)
+            part = heard_power(forms[block, 0:size], entry_rows, entry_heard - first_cell, count, step)
+            total = total + jnp.where(entry_block == block, part, 0.0)
+        return total
+
+    far = half * (1 - near)
+    for offset in range(1, half):
+        w_copies[offset].wait_recv()
+    entry_power = add_powers(half * near, half, 1, False, hand_on)
+    entry_power = entry_power + add_powers(far + parity, half // 2, 2, True, None)
+    for offset in range(half + 1, groups, 2):
+        w_copies[offset].wait_recv()
+    entry_power = entry_power + add_powers(far + 1 - parity, half // 2, 2, True, None)
 
     for copy in sc_copies:
         copy.wait_recv()
@@ -511,7 +541,7 @@
         power = received[block] * scales[0]
         metric_ref[block : block + 1, :] = jnp.log2(1.0 + power / (interference + floor))
 
-    for copy in row_copies + more_copies + pw_copies + w_copies + sc_copies:
+    for copy in row_copies + more_copies + pw_copies + list(w_copies.values()) + sc_copies:
         copy.wait_send()
 
 
@@ -564,8 +594,8 @@
             pltpu.VMEM((groups, capacity, width), BF16),
             pltpu.VMEM((groups, capacity, (slots - 1) * width), BF16),
             pltpu.VMEM((groups, capacity, (slots - 1) * width), BF16),
-            pltpu.VMEM((groups, 8, width), F32),
-            pltpu.VMEM((groups, 8, width), F32),
+            pltpu.VMEM((groups, slots - 1, width), F32),
+            pltpu.VMEM((groups, slots - 1, width), F32),
             pltpu.VMEM((entries, width), BF16),
             pltpu.VMEM((groups, entries, width), BF16),
             pltpu.VMEM((blocks, cells * beams, width), BF16),

time: 28 us -> 28.8 us (1.029)
  Pallas kernels: 27.1 us -> 27.9 us
    pallas_call x1, Pallas kernels: 25.7 us -> 26.5 us  [on_device(): pl.pallas_call(functools.partial(kernel, dims), out_shape=results, in_spe...]
where the time goes in v5:
time: 28.8 us; the launch traced here: 28.6 us
  Pallas kernels  27.9 us (97%)
  between operations  0.64 us (2%)
    pallas_call x1, Pallas kernels, on_device(): pl.pallas_call(functools.partial(kernel, dims), out_shape=results, in_spe...  26.5 us
    pallas_call x1, Pallas kernels, on_device(): pl.pallas_call(hand_over, out_shape=results, in_specs=[vmem] * 3, out_spe...  1.42 us

profile of v5, /device:TPU:0, one launch (start us, length us, event | category | flops | bytes accessed | tf_op | source)
XLA Modules:
  0.0 28.6 jit_solution(7871807292562708871)
XLA Ops:
  0.6 26.5 %shard_map.85 = (bf16[128,128]{1,0:T(8,128)(2,1)}, f32[4,1024]{1,0:T(4,128)}, f32[2,4,16]{2,1,0:T(4,128)}) custom-call(bf16[12288,128]{1,0:T(8,128)(2,1)} %bitcast.7, s32[16,4,16]{2,1,0:T(4,128)} %plan_hbm.1, s32[1,1024]{1,0:T(1,128)} %bitcast.9, s32[2,1024]{1,0:T(2,128)} %bitcast.8, f32[2]{0:T(128)} %reg_hbm.1, f32[16]{0:T(128)} %noise_hbm.1), custom_call_target="tpu_custom_call" | custom-call | tf_op jit(solution)/shard_map/pallas_call | solution.py:579
  27.2 1.4 %shard_map.86 = (bf16[128,128]{1,0:T(8,128)(2,1)}, f32[4,1024]{1,0:T(4,128)}, f32[2,4,16]{2,1,0:T(4,128)}) custom-call(bf16[128,128]{1,0:T(8,128)(2,1)} %get-tuple-element.9.refs_0_, f32[4,1024]{1,0:T(4,128)} %get-tuple-element.10.refs_1_, f32[2,4,16]{2,1,0:T(4,128)} %get-tuple-element.11.refs_2_), custom_call_target="tpu_custom_call" | custom-call | tf_op jit(solution)/shard_map/pallas_call | solution.py:619

commit v6 on v3

--- a/solution.py
+++ b/solution.py
@@ -125,6 +125,7 @@
     noise_ref,
     wide,
     planes,
+    columns,
     out_rows,
     in_rows,
     out_more,
@@ -301,7 +302,7 @@
     for group in range(groups):
         part = slice(group * capacity, (group + 1) * capacity)
         out_more[group] = gathered[part].astype(BF16)
-        out_ids[group, :, 0:capacity] = ids[:, part]
+        out_ids[group, :, 0:capacity] = ids[0 : slots - 1, part]
     more_copies = []
     for offset in range(1, groups):
         dst = flip(me, offset, groups)
@@ -382,6 +383,14 @@
         copy.start()
         pw_copies.append(copy)
     pw_in[pl.ds(my_rb, 1)] = pw_own[...][None]
+
+    def turn_over(slot, carry):
+        for block in range(blocks):
+            number = slot * blocks + block
+            columns[number] = jnp.transpose(planes[number])
+        return carry
+
+    lax.fori_loop(0, slots, turn_over, 0)
     for copy in pw_copies:
         copy.wait_recv()
     total = jnp.sum(jnp.sum(pw_in[...], axis=0), axis=1, keepdims=True)
@@ -416,8 +425,9 @@
     more = dot_nn(place, came.astype(BF16))
     entry_rows = jnp.concatenate(
         [more[:, slot * width : (slot + 1) * width] for slot in range(slots - 1)], axis=0
-    ).astype(BF16)
-    entry_ids = jnp.zeros((8, entries), F32)
+    )
+    entry_rows = jnp.transpose(entry_rows).astype(BF16)
+    entry_ids = jnp.zeros((slots - 1, entries), F32)
     for group in range(groups):
         known = in_ids[group, :, 0:capacity].astype(BF16)
         entry_ids = entry_ids + dot_nn(known, arrivals[group].astype(BF16))
@@ -433,8 +443,8 @@
     form_rows = 2 * part_rows
 
     def heard_power(form, rows, heard):
-        lanes = rows.shape[0]
-        projected = dot_nt(form, rows)
+        lanes = rows.shape[1]
+        projected = dot_nn(form, rows)
         energy = jnp.sum(
             (projected * projected).reshape(half, form_rows // 8, 8, lanes), axis=1
         )
@@ -463,7 +473,7 @@
             heard = cells_ref[slot] - first_cell
             for block in range(blocks):
                 number = slot * blocks + block
-                part = heard_power(forms[block], planes[number], heard)
+                part = heard_power(forms[block], columns[number], heard)
                 received[number] = received[number] + part if keep else part
             return carry
 
@@ -560,12 +570,13 @@
             pltpu.SMEM(noise_floor.shape, F32),
             pltpu.VMEM((row_count, width), F32),
             pltpu.VMEM((slots * blocks, tracks, width), BF16),
+            pltpu.VMEM((slots * blocks, width, tracks), BF16),
             pltpu.VMEM((groups, capacity, width), BF16),
             pltpu.VMEM((groups, capacity, width), BF16),
             pltpu.VMEM((groups, capacity, (slots - 1) * width), BF16),
             pltpu.VMEM((groups, capacity, (slots - 1) * width), BF16),
-            pltpu.VMEM((groups, 8, width), F32),
-            pltpu.VMEM((groups, 8, width), F32),
+            pltpu.VMEM((groups, slots - 1, width), F32),
+            pltpu.VMEM((groups, slots - 1, width), F32),
             pltpu.VMEM((entries, width), BF16),
             pltpu.VMEM((groups, entries, width), BF16),
             pltpu.VMEM((blocks, cells * beams, width), BF16),

time: 28 us -> 27.9 us (level)
  no operation moved by 1% of the time
where the time goes in v6:
time: 27.9 us; the launch traced here: 27.7 us
  Pallas kernels  27 us (97%)
  between operations  0.64 us (2%)
    pallas_call x1, Pallas kernels, on_device(): pl.pallas_call(functools.partial(kernel, dims), out_shape=results, in_spe...  25.6 us
    pallas_call x1, Pallas kernels, on_device(): pl.pallas_call(hand_over, out_shape=results, in_specs=[vmem] * 3, out_spe...  1.42 us

profile of v6, /device:TPU:0, one launch (start us, length us, event | category | flops | bytes accessed | tf_op | source)
XLA Modules:
  0.0 27.7 jit_solution(5660503942219465733)
XLA Ops:
  0.6 25.6 %shard_map.85 = (bf16[128,128]{1,0:T(8,128)(2,1)}, f32[4,1024]{1,0:T(4,128)}, f32[2,4,16]{2,1,0:T(4,128)}) custom-call(bf16[12288,128]{1,0:T(8,128)(2,1)} %bitcast.7, s32[16,4,16]{2,1,0:T(4,128)} %plan_hbm.1, s32[1,1024]{1,0:T(1,128)} %bitcast.9, s32[2,1024]{1,0:T(2,128)} %bitcast.8, f32[2]{0:T(128)} %reg_hbm.1, f32[16]{0:T(128)} %noise_hbm.1), custom_call_target="tpu_custom_call" | custom-call | tf_op jit(solution)/shard_map/pallas_call | solution.py:559
  26.2 1.4 %shard_map.86 = (bf16[128,128]{1,0:T(8,128)(2,1)}, f32[4,1024]{1,0:T(4,128)}, f32[2,4,16]{2,1,0:T(4,128)}) custom-call(bf16[128,128]{1,0:T(8,128)(2,1)} %get-tuple-element.9.refs_0_, f32[4,1024]{1,0:T(4,128)} %get-tuple-element.10.refs_1_, f32[2,4,16]{2,1,0:T(4,128)} %get-tuple-element.11.refs_2_), custom_call_target="tpu_custom_call" | custom-call | tf_op jit(solution)/shard_map/pallas_call | solution.py:600

commit v7 on v3

--- a/solution.py
+++ b/solution.py
@@ -203,6 +203,19 @@
             device_id_type=pl.DeviceIdType.MESH,
         )
 
+    stride = slots * blocks
+    for i in range(pieces):
+        loads[i].wait()
+        part = slice(i * chunk, (i + 1) * chunk)
+        wide[part, :] = raw[part, :].astype(F32)
+
+    def extract(slot):
+        for block in range(blocks):
+            number = slot * blocks + block
+            planes[number] = wide[pl.ds(number, tracks, stride=stride), :].astype(BF16)
+
+    extract(0)
+
     for copy in small:
         copy.wait()
     for slot in range(1, slots):
@@ -211,21 +224,21 @@
     spread_plan = None
     for block in range(blocks):
         lane = iota((beams, entries), 1) & (cell_lanes - 1)
-        put = jnp.where(lane == iota((beams, entries), 0) + block * beams, 1.0, 0.0)
-        part = jnp.dot(
-            plan_ref[:, block, :].astype(F32), put, precision=HIGH, preferred_element_type=F32
-        )
+        put = jnp.where(lane == iota((beams, entries), 0) + block * beams, 1.0, 0.0).astype(BF16)
+        entry = plan_ref[:, block, :]
+        halves = jnp.concatenate([entry >> 8, entry & 255], axis=0).astype(F32).astype(BF16)
+        part = dot_nn(halves, put)
         spread_plan = part if spread_plan is None else spread_plan + part
     ent_f = jnp.zeros((groups, entries), F32)
     for cell in range(cell_dev):
         pick = jnp.where(
             iota((groups, cells), 1) == cell_dev * iota((groups, cells), 0) + cell, 1.0, 0.0
-        )
+        ).astype(BF16)
         lane = iota((cells, entries), 1)
         in_cell = (lane >= cell * cell_lanes) & (lane < (cell + 1) * cell_lanes)
-        ent_f = ent_f + jnp.dot(
-            pick, jnp.where(in_cell, spread_plan, 0.0), precision=HIGH, preferred_element_type=F32
-        )
+        high = jnp.where(in_cell, spread_plan[0:cells], 0.0).astype(BF16)
+        low = jnp.where(in_cell, spread_plan[cells : 2 * cells], 0.0).astype(BF16)
+        ent_f = ent_f + (256.0 * dot_nn(pick, high) + dot_nn(pick, low))
     ent = ent_f.astype(jnp.int32)
 
     owner = ent >> track_shift
@@ -251,19 +264,6 @@
         ],
         axis=0,
     ).astype(jnp.int32) - 1
-
-    stride = slots * blocks
-    for i in range(pieces):
-        loads[i].wait()
-        part = slice(i * chunk, (i + 1) * chunk)
-        wide[part, :] = raw[part, :].astype(F32)
-
-    def extract(slot):
-        for block in range(blocks):
-            number = slot * blocks + block
-            planes[number] = wide[pl.ds(number, tracks, stride=stride), :].astype(BF16)
-
-    extract(0)
 
     track_lane = iota((groups * capacity, tracks), 1)
     gathered = None
@@ -301,7 +301,7 @@
     for group in range(groups):
         part = slice(group * capacity, (group + 1) * capacity)
         out_more[group] = gathered[part].astype(BF16)
-        out_ids[group, :, 0:capacity] = ids[:, part]
+        out_ids[group, :, 0:capacity] = ids[0 : slots - 1, part]
     more_copies = []
     for offset in range(1, groups):
         dst = flip(me, offset, groups)
@@ -417,7 +417,7 @@
     entry_rows = jnp.concatenate(
         [more[:, slot * width : (slot + 1) * width] for slot in range(slots - 1)], axis=0
     ).astype(BF16)
-    entry_ids = jnp.zeros((8, entries), F32)
+    entry_ids = jnp.zeros((slots - 1, entries), F32)
     for group in range(groups):
         known = in_ids[group, :, 0:capacity].astype(BF16)
         entry_ids = entry_ids + dot_nn(known, arrivals[group].astype(BF16))
@@ -443,8 +443,25 @@
         found = jnp.sum(jnp.where(cell == heard[None], energy, 0.0), axis=0)
         return jnp.sum(found, axis=0, keepdims=True)
 
+    floor = jnp.zeros((1, tracks), F32)
+    serving = cells_ref[0]
+    for cell in range(cells):
+        floor = jnp.where(serving == cell, noise_ref[cell], floor)
+    def scale_row(heard):
+        row = jnp.zeros(heard.shape, F32)
+        for group in range(groups):
+            for cell in range(cell_dev):
+                one = sc_in[group, cell : cell + 1, 0:1]
+                row = jnp.where(heard == group * cell_dev + cell, one, row)
+        return row
+
     entry_power = jnp.zeros((1, entry_lanes), F32)
     for turn_number in range(2):
+        if turn_number == 1:
+            for copy in sc_copies:
+                copy.wait_recv()
+            scales = [scale_row(cells_ref[slot]) for slot in range(slots)]
+            entry_scale = scale_row(entry_heard)
         for offset in range(1, groups):
             if offset // half == turn_number:
                 w_copies[offset - 1].wait_recv()
@@ -472,18 +489,7 @@
             part = heard_power(forms[block], entry_rows, entry_heard - first_cell)
             entry_power = entry_power + jnp.where(entry_block == block, part, 0.0)
 
-    for copy in sc_copies:
-        copy.wait_recv()
-
-    def scale_row(heard):
-        row = jnp.zeros(heard.shape, F32)
-        for group in range(groups):
-            for cell in range(cell_dev):
-                one = sc_in[group, cell : cell + 1, 0:1]
-                row = jnp.where(heard == group * cell_dev + cell, one, row)
-        return row
-
-    entry_power = entry_power * scale_row(entry_heard)
+    entry_power = entry_power * entry_scale
     entry_denominator = entry_power[:, 0:entries]
     for slot in range(1, slots - 1):
         entry_denominator = entry_denominator + entry_power[:, slot * entries : (slot + 1) * entries]
@@ -499,11 +505,6 @@
             start = (cell * blocks + block) * beams
             rate_ref[cell, block : block + 1, :] = rate[:, start : start + beams]
 
-    scales = [scale_row(cells_ref[slot]) for slot in range(slots)]
-    floor = jnp.zeros((1, tracks), F32)
-    serving = cells_ref[0]
-    for cell in range(cells):
-        floor = jnp.where(serving == cell, noise_ref[cell], floor)
     for block in range(blocks):
         interference = received[blocks + block] * scales[1]
         for slot in range(2, slots):
@@ -564,8 +565,8 @@
             pltpu.VMEM((groups, capacity, width), BF16),
             pltpu.VMEM((groups, capacity, (slots - 1) * width), BF16),
             pltpu.VMEM((groups, capacity, (slots - 1) * width), BF16),
-            pltpu.VMEM((groups, 8, width), F32),
-            pltpu.VMEM((groups, 8, width), F32),
+            pltpu.VMEM((groups, slots - 1, width), F32),
+            pltpu.VMEM((groups, slots - 1, width), F32),
             pltpu.VMEM((entries, width), BF16),
             pltpu.VMEM((groups, entries, width), BF16),
             pltpu.VMEM((blocks, cells * beams, width), BF16),

time: 28 us -> 28.2 us (level)
  no operation moved by 1% of the time
where the time goes in v7:
time: 28.2 us; the launch traced here: 27.9 us
  Pallas kernels  27.3 us (97%)
  between operations  0.64 us (2%)
    pallas_call x1, Pallas kernels, on_device(): pl.pallas_call(functools.partial(kernel, dims), out_shape=results, in_spe...  25.9 us
    pallas_call x1, Pallas kernels, on_device(): pl.pallas_call(hand_over, out_shape=results, in_specs=[vmem] * 3, out_spe...  1.42 us

profile of v7, /device:TPU:0, one launch (start us, length us, event | category | flops | bytes accessed | tf_op | source)
XLA Modules:
  0.0 27.9 jit_solution(2324259969671305042)
XLA Ops:
  0.6 25.9 %shard_map.85 = (bf16[128,128]{1,0:T(8,128)(2,1)}, f32[4,1024]{1,0:T(4,128)}, f32[2,4,16]{2,1,0:T(4,128)}) custom-call(bf16[12288,128]{1,0:T(8,128)(2,1)} %bitcast.7, s32[16,4,16]{2,1,0:T(4,128)} %plan_hbm.1, s32[1,1024]{1,0:T(1,128)} %bitcast.9, s32[2,1024]{1,0:T(2,128)} %bitcast.8, f32[2]{0:T(128)} %reg_hbm.1, f32[16]{0:T(128)} %noise_hbm.1), custom_call_target="tpu_custom_call" | custom-call | tf_op jit(solution)/shard_map/pallas_call | solution.py:550
  26.5 1.4 %shard_map.86 = (bf16[128,128]{1,0:T(8,128)(2,1)}, f32[4,1024]{1,0:T(4,128)}, f32[2,4,16]{2,1,0:T(4,128)}) custom-call(bf16[128,128]{1,0:T(8,128)(2,1)} %get-tuple-element.9.refs_0_, f32[4,1024]{1,0:T(4,128)} %get-tuple-element.10.refs_1_, f32[2,4,16]{2,1,0:T(4,128)} %get-tuple-element.11.refs_2_), custom_call_target="tpu_custom_call" | custom-call | tf_op jit(solution)/shard_map/pallas_call | solution.py:590
